TPU v7x, 32 devices: a whole 2x2x4 slice. The times are simulated.
32 devices in a mesh: dom: 32 (over z, y, x, core).
Axes of the slice: x: 2, y: 2, z: 4, core: 2. Of those that a mesh axis runs over, the one named last changes fastest.
Arguments:
- ham_core: float32 [20480, 1280], P('dom')
- halo_rows: float32 [32, 8, 80, 1280], P('dom'), as said below
- halo_request: int32 [32, 160], P('dom'), may hold values from -1 to 159, as said below
- deriv: float32 [3, 5120, 4, 1280], P(None, 'dom'), may hold values from -15 to 15
- e_low: float32 [1], replicated, may hold values from -8 to -5
- e_high: float32 [1], replicated, may hold values from 4.5 to 7.5
- branches: int32 [5], replicated, may hold values from 0 to 1
Outputs:
- density: float32 [20480, 1280], P('dom')
- forces: float32 [3, 5120], P(None, 'dom')
Inputs may be any that keep to these rules, and one draw needn't show every extreme that they name: Entry halo_request[d, k * 20 + s] is an atom index of the owner of block k of d, or -1 for an empty slot; in each block of 20 the live entries come first and are distinct; in every draw some partition asks 20 atoms of each of its 8 neighbours and is asked 20 atoms by each of them. For c < 640: halo_rows[p, k, r, c] equals ham_core[d * 640 + c, 640 + 4 * 20 * k + r] with d = (p - off_k) mod 32.
All inputs are finite; a program needn't handle non-finite values.
Results may differ from a plain program's by a relative error of at most 0.0003.
Values sent between devices are 32-bit elements; how exact they have to be, the bound alone decides.
No kernel may reach another device: no remote copies, remote signals or barrier semaphores. Data moves between devices by JAX's collectives and lax.ppermute only.
A program may use at most 128 MiB of HBM per device.

v0:
```python
import functools

import jax
import jax.numpy as jnp
from jax import lax
from jax.experimental import pallas as pl
from jax.experimental.pallas import tpu as pltpu
from jax.sharding import PartitionSpec as P

ORB = 4
NB = 4
ITERS = 5
PANEL = 256
SUB = 128
VMEM_BYTES = 38 * 1024 * 1024
OWN_VMEM_BYTES = 16 * 1024 * 1024


def passed_along(value, axis, steps):
    count = lax.axis_size(axis)
    pairs = [(source, (source + steps) % count) for source in range(count)]
    return lax.ppermute(value, axis, pairs)


def block_offset(block):
    if block < NB:
        return block + 1
    return NB - 1 - block


def halves(value):
    high = value.astype(jnp.bfloat16)
    low = (value - high.astype(jnp.float32)).astype(jnp.bfloat16)
    return high, low


def thirds(value):
    high = value.astype(jnp.bfloat16)
    rest = value - high.astype(jnp.float32)
    middle, low = halves(rest)
    return high, middle, low


def dot(left, right):
    return jnp.dot(left, right, preferred_element_type=jnp.float32)


def dot_one_hot(value, one_hot):
    return sum(dot(part, one_hot) for part in thirds(value))


def on_diagonal(shape):
    return lax.broadcasted_iota(jnp.int32, shape, 0) == lax.broadcasted_iota(jnp.int32, shape, 1)


def three_passes(left_high, left_low, right_high, right_low):
    return dot(
        jnp.concatenate([left_high, left_high, left_low], axis=1),
        jnp.concatenate([right_high, right_low, right_high], axis=0),
    )


def square_passes(left_high, left_low, right_high, right_low):
    cross = dot(left_high, right_low)
    return dot(left_high, right_high) + (cross + cross.T)


def step_factors(branches, number):
    taken = (branches[number] == 1).astype(jnp.float32)
    return 2.0 * taken, 1.0 - 2.0 * taken


def panels(start, end):
    cuts = [start] + [at for at in range(0, end, PANEL) if at > start] + [end]
    return [slice(low, high) for low, high in zip(cuts, cuts[1:])]


def spread_lanes(column, width):
    return jnp.concatenate([column] * (width // SUB), axis=1)


def combined(old, off, keep, add, state, rows_at, cols_at, on_diag):
    diag_row, diag_col = state[2:]
    factor_col = spread_lanes(keep + add * diag_col[rows_at, :], old.shape[1])
    value = old * (factor_col + add * diag_row[0:1, cols_at]) + add * off
    if on_diag:
        value = value - jnp.where(on_diagonal(value.shape), add * (old * old), 0.0)
    return value


def store_matrix(value, state, rows_at, cols_at):
    high_ref, low_ref, diag_row, diag_col = state
    if rows_at.start == cols_at.start:
        size = value.shape[0]
        line = jnp.where(on_diagonal(value.shape), value, 0.0)
        diag_row[:, cols_at] = jnp.broadcast_to(jnp.sum(line, axis=0, keepdims=True), (8, size))
        diag_col[rows_at, :] = jnp.broadcast_to(jnp.sum(line, axis=1, keepdims=True), (size, SUB))
        value = value - line
    high, low = halves(value)
    high_ref[rows_at, cols_at] = high
    low_ref[rows_at, cols_at] = low
    if rows_at.start != cols_at.start:
        high_ref[cols_at, rows_at] = high.T
        low_ref[cols_at, rows_at] = low.T


def start_block(source, row, col, top, scale):
    value = 0.5 * (source[row, col] + source[col, row].T)
    if row.start == col.start:
        value = value - jnp.where(on_diagonal(value.shape), top, 0.0)
    return -scale * value


def cut(size):
    return [slice(at, at + SUB) for at in range(0, size, SUB)]


def shifted(piece, by):
    return slice(piece.start + by, piece.stop + by)


def asked_atoms(request, orbitals):
    atoms = request.shape[1]
    expand = lax.broadcasted_iota(jnp.int32, (orbitals, atoms), 0) // ORB == lax.broadcasted_iota(
        jnp.int32, (orbitals, atoms), 1
    )
    expand = expand.astype(jnp.float32).astype(jnp.bfloat16)
    values = jnp.broadcast_to(request[...].astype(jnp.float32), (8, atoms)).astype(jnp.bfloat16)
    transposed = (((1,), (1,)), ((), ()))
    row = lax.dot_general(values, expand, transposed, preferred_element_type=jnp.float32)
    col = lax.dot_general(expand, values, transposed, preferred_element_type=jnp.float32)
    return row[0:1, :], col[:, 0:1]


def own_kernel(
    high_end, low_end, branches, core, request, high_cross, low_cross, x_cross, y_cross, y_halo,
    x_own, next_high, next_low, next_col, next_row, high, low, diag_row, diag_col
):
    rows, order = core.shape
    state = (high, low, diag_row, diag_col)
    later = (next_high, next_low, next_row, next_col)
    left, right = slice(0, rows), slice(rows, order)
    top = high_end[0]
    scale = 1.0 / (high_end[0] - low_end[0])
    keep, add = step_factors(branches, 0)
    asked_row, _ = asked_atoms(request, order - rows)
    live_row = (asked_row >= 0).astype(jnp.float32)
    for row in cut(rows):
        for col in cut(order - rows):
            value = -scale * (core[row, shifted(col, rows)] * live_row[:, col])
            x_cross[row, col] = value
            store_matrix(value, state, row, shifted(col, rows))
    for row in cut(rows):
        for col in cut(rows):
            if row.start <= col.start:
                value = start_block(core, row, col, top, scale)
                x_own[row, col] = value
                if row.start < col.start and row.start // PANEL == col.start // PANEL:
                    x_own[col, row] = value.T
                store_matrix(value, state, row, col)
    high_cross[...] = high[left, right]
    low_cross[...] = low[left, right]
    for row in panels(0, rows):
        for col in panels(rows, order):
            at = shifted(col, -rows)
            off = three_passes(high[row, left], low[row, left], high[left, col], low[left, col])
            factor = spread_lanes(keep + add * diag_col[row, :], at.stop - at.start)
            y_cross[row, at] = x_cross[row, at] * factor + add * off
    for row in panels(rows, order):
        for col in panels(rows, order):
            if row.start <= col.start:
                passes = square_passes if row.start == col.start else three_passes
                off = passes(high[row, left], low[row, left], high[left, col], low[left, col])
                y_halo[shifted(row, -rows), shifted(col, -rows)] = add * off
    for row in panels(0, rows):
        for col in panels(0, rows):
            if row.start <= col.start:
                passes = square_passes if row.start == col.start else three_passes
                off = passes(high[row, :], low[row, :], high[:, col], low[:, col])
                value = combined(
                    x_own[row, col], off, keep, add, state, row, col, row.start == col.start
                )
                x_own[row, col] = value
                store_matrix(value, later, row, col)


def kernel(place, high_end, low_end, branches, request, *refs):
    deriv, refs = refs[:3], refs[3:]
    block_count = 2 * NB
    (high_cross, low_cross, x_cross, y_cross, y_halo, x_own, high_own, low_own, own_col, own_row) = refs[:10]
    pieces = refs[10 : 10 + block_count]
    density_out, own_out, mail = refs[10 + block_count : 13 + block_count]
    (x, high_a, low_a, high_b, low_b, diag_row_a, diag_row_b, diag_col_a, diag_col_b) = refs[
        13 + block_count : 22 + block_count
    ]
    halo, deriv_held, row_part, deriv_sems, out_sem = refs[22 + block_count :]
    order = x.shape[0]
    rows = x_own.shape[0]
    atoms = rows // ORB
    slot_rows = (order - rows) // block_count
    left, right = slice(0, rows), slice(rows, order)

    deriv_copies = [
        pltpu.make_async_copy(deriv[c], deriv_held.at[c], deriv_sems.at[c]) for c in range(3)
    ]
    for copy in deriv_copies:
        copy.start()
    state_a = (high_a, low_a, diag_row_a, diag_col_a)
    state_b = (high_b, low_b, diag_row_b, diag_col_b)

    top = high_end[0]
    scale = 1.0 / (high_end[0] - low_end[0])
    for block in range(block_count):
        halo[block * slot_rows : (block + 1) * slot_rows, :] = pieces[block][...]
    asked_row, asked_col = asked_atoms(request, order - rows)
    live_row = (asked_row >= 0).astype(jnp.float32)
    live_col = (asked_col >= 0).astype(jnp.float32)
    for row in cut(order - rows):
        for col in cut(order - rows):
            if row.start <= col.start:
                value = start_block(halo, row, col, top, scale)
                value = value * live_col[row, :] * live_row[:, col]
                down, across = shifted(row, rows), shifted(col, rows)
                x[down, across] = value
                if row.start < col.start and down.start // PANEL == across.start // PANEL:
                    x[across, down] = value.T
                store_matrix(value, state_b, row, col)
    x[left, left] = x_own[...]
    high_a[left, left] = high_own[...]
    low_a[left, left] = low_own[...]
    diag_col_a[left, :] = own_col[...]
    diag_row_a[:, left] = own_row[...]
    keep, add = step_factors(branches, 0)
    for row in panels(0, rows):
        for col in panels(rows, order):
            at = shifted(col, -rows)
            off = three_passes(high_cross[row, :], low_cross[row, :], high_b[left, at], low_b[left, at])
            value = y_cross[row, at] + x_cross[row, at] * (add * diag_row_b[0:1, at]) + add * off
            x[row, col] = value
            if row.start // PANEL == col.start // PANEL:
                x[col, row] = value.T
            store_matrix(value, state_a, row, col)
    for row in panels(rows, order):
        for col in panels(rows, order):
            if row.start <= col.start:
                down, across = shifted(row, -rows), shifted(col, -rows)
                passes = square_passes if row.start == col.start else three_passes
                off = passes(high_b[down, left], low_b[down, left], high_b[left, across], low_b[left, across])
                on_diag = row.start == col.start
                value = combined(x[row, col], off, keep, add, state_b, down, across, on_diag)
                value = value + y_halo[down, across]
                x[row, col] = value
                store_matrix(value, state_a, row, col)

    def block_step(number, now, later, lines, cols):
        keep, add = step_factors(branches, number)
        high, low = now[:2]
        on_diag = lines.start == cols.start
        passes = square_passes if on_diag else three_passes
        off = passes(high[lines, :], low[lines, :], high[:, cols], low[:, cols])
        value = combined(x[lines, cols], off, keep, add, now, lines, cols, on_diag)
        x[lines, cols] = value
        store_matrix(value, later, lines, cols)

    def squaring(number, now, later, unless_last):
        away = []
        for cols in panels(0, order):
            for lines in panels(0, cols.stop):
                if lines.start >= rows:
                    away.append((lines, cols))
                else:
                    block_step(number, now, later, lines, cols)

        def others():
            for lines, cols in away:
                block_step(number, now, later, lines, cols)

        if unless_last:
            pl.when(number < ITERS - 1)(others)
        else:
            others()

    def two(pair, carry):
        squaring(2 * pair + 1, state_a, state_b, False)
        squaring(2 * pair + 2, state_b, state_a, True)
        return carry

    lax.fori_loop(0, (ITERS - 1) // 2, two, 0)
    for cols in panels(0, rows):
        for lines in panels(0, cols.start) if cols.start > 0 else []:
            x[cols, lines] = x[lines, cols].T

    out_copy = pltpu.make_async_copy(x.at[left, :], density_out, out_sem)
    out_copy.start()

    chunk = 64
    line = lax.broadcasted_iota(jnp.int32, (8, order), 0)
    columns = jnp.zeros((8, order), jnp.float32)
    own_rows = jnp.zeros((8, rows), jnp.float32)
    ones = jnp.ones((8, SUB), jnp.bfloat16)
    for c in range(3):
        deriv_copies[c].wait()

        def strip(number, total, c=c):
            at = pl.ds(pl.multiple_of(number * chunk, chunk), chunk)
            weighted = x[at, :] * deriv_held[c, at, :]
            row_part[at, :] = sum(weighted[:, lane : lane + SUB] for lane in range(0, order, SUB))
            return total + jnp.sum(weighted.reshape(chunk // 8, 8, order), axis=0)

        total = lax.fori_loop(0, rows // chunk, strip, jnp.zeros((8, order), jnp.float32))
        columns = jnp.where(line == c, jnp.sum(total, axis=0, keepdims=True), columns)
        row_sums = sum(
            lax.dot_general(ones, part, (((1,), (1,)), ((), ())), preferred_element_type=jnp.float32)
            for part in thirds(row_part[...])
        )
        own_rows = jnp.where(line[:, :rows] == c, row_sums, own_rows)
    atom_ids = lax.broadcasted_iota(jnp.int32, (rows, atoms), 1)
    own_hot = (lax.broadcasted_iota(jnp.int32, (rows, atoms), 0) // ORB == atom_ids).astype(jnp.float32)
    own_out[...] = dot_one_hot(2.0 * (own_rows - columns[:, :rows]), own_hot.astype(jnp.bfloat16))
    letter = jnp.where(line[:, rows:] == 3, asked_row, -2.0 * columns[:, rows:])
    empty = jnp.where(lax.broadcasted_iota(jnp.int32, (4, SUB - slot_rows), 0) == 3, -1.0, 0.0)
    mail[...] = jnp.zeros(mail.shape, jnp.float32)
    for block in range(block_count):
        content = letter[0:4, block * slot_rows : (block + 1) * slot_rows]
        to = lax.rem(place[0] + (block_offset(block) + mail.shape[0]), mail.shape[0])
        mail[to] = jnp.concatenate([content, empty], axis=1)
    out_copy.wait()


def collect(place, mail, own, forces):
    count = mail.shape[0]
    atoms = own.shape[1]
    letters = jnp.concatenate(
        [mail[lax.rem(place[0] + (count - block_offset(block)), count)] for block in range(2 * NB)],
        axis=1,
    )
    wanted = letters[3:4, :] == lax.broadcasted_iota(jnp.int32, (atoms, 1), 0).astype(jnp.float32)
    wanted = wanted.astype(jnp.float32).astype(jnp.bfloat16)
    sums = sum(
        lax.dot_general(part, wanted, (((1,), (1,)), ((), ())), preferred_element_type=jnp.float32)
        for part in thirds(jnp.concatenate([letters, letters], axis=0))
    )
    forces[...] = own[0:3, :] + sums[0:3, :]


def own_part(high_end, low_end, branches, core, request):
    rows, order = core.shape
    halo = order - rows
    vmem = pl.BlockSpec(memory_space=pltpu.VMEM)
    smem = pl.BlockSpec(memory_space=pltpu.SMEM)
    kinds = [
        ((rows, halo), jnp.bfloat16),
        ((rows, halo), jnp.bfloat16),
        ((rows, halo), jnp.float32),
        ((rows, halo), jnp.float32),
        ((halo, halo), jnp.float32),
        ((rows, rows), jnp.float32),
        ((rows, rows), jnp.bfloat16),
        ((rows, rows), jnp.bfloat16),
        ((rows, SUB), jnp.float32),
        ((8, rows), jnp.float32),
    ]
    return pl.pallas_call(
        own_kernel,
        out_shape=[jax.ShapeDtypeStruct(*kind) for kind in kinds],
        in_specs=[smem, smem, smem, vmem, vmem],
        out_specs=[vmem] * len(kinds),
        scratch_shapes=[
            pltpu.VMEM((order, order), jnp.bfloat16),
            pltpu.VMEM((order, order), jnp.bfloat16),
            pltpu.VMEM((8, order), jnp.float32),
            pltpu.VMEM((order, SUB), jnp.float32),
        ],
        compiler_params=pltpu.CompilerParams(vmem_limit_bytes=OWN_VMEM_BYTES),
        cost_estimate=pl.CostEstimate(
            flops=2 * 3 * order**3 // 3, bytes_accessed=13_000_000, transcendentals=0
        ),
    )(high_end, low_end, branches, core, request)


def density_and_terms(place, high_end, low_end, branches, request, deriv, ready, pieces):
    rows, order = deriv[0].shape
    atoms = rows // ORB
    vmem = pl.BlockSpec(memory_space=pltpu.VMEM)
    smem = pl.BlockSpec(memory_space=pltpu.SMEM)
    anywhere = pl.BlockSpec(memory_space=pl.ANY)
    square = (order, order)
    return pl.pallas_call(
        kernel,
        out_shape=[
            jax.ShapeDtypeStruct((rows, order), jnp.float32),
            jax.ShapeDtypeStruct((8, atoms), jnp.float32),
            jax.ShapeDtypeStruct((lax.axis_size("dom"), 4, SUB), jnp.float32),
        ],
        in_specs=[smem, smem, smem, smem, vmem] + [anywhere] * 3 + [vmem] * (len(ready) + len(pieces)),
        out_specs=[anywhere, vmem, vmem],
        scratch_shapes=[
            pltpu.VMEM(square, jnp.float32),
            pltpu.VMEM(square, jnp.bfloat16),
            pltpu.VMEM(square, jnp.bfloat16),
            pltpu.VMEM(square, jnp.bfloat16),
            pltpu.VMEM(square, jnp.bfloat16),
            pltpu.VMEM((8, order), jnp.float32),
            pltpu.VMEM((8, order), jnp.float32),
            pltpu.VMEM((order, SUB), jnp.float32),
            pltpu.VMEM((order, SUB), jnp.float32),
            pltpu.VMEM((order - rows, order - rows), jnp.float32),
            pltpu.VMEM((3, rows, order), jnp.float32),
            pltpu.VMEM((rows, SUB), jnp.float32),
            pltpu.SemaphoreType.DMA((3,)),
            pltpu.SemaphoreType.DMA,
        ],
        compiler_params=pltpu.CompilerParams(vmem_limit_bytes=VMEM_BYTES),
        cost_estimate=pl.CostEstimate(
            flops=2 * 3 * 3 * order**3, bytes_accessed=24_000_000, transcendentals=0
        ),
    )(place, high_end, low_end, branches, request, *deriv, *ready, *pieces)


def per_device(ham_core, halo_rows, halo_request, deriv, e_low, e_high, branches):
    row_count, order_all = ham_core.shape
    block_count = 2 * NB
    early = (6, 3, 2, 1, 5)
    late = (0, 4, 7)
    first = halo_rows[0, early[0], :, row_count:]
    pieces = {early[0]: passed_along(first, "dom", -block_offset(early[0]))}
    rest, _ = lax.optimization_barrier((halo_rows, first))
    halo = rest[0, :, :, row_count:]
    for block in early[1:]:
        pieces[block] = passed_along(halo[block], "dom", -block_offset(block))
    ready = own_part(e_high, e_low, branches, ham_core, halo_request)
    flat_deriv = [deriv[c].reshape(row_count, order_all) for c in range(3)]
    waiting, ready, flat_deriv[0] = lax.optimization_barrier(
        ([halo[block] for block in late], ready, flat_deriv[0])
    )
    for block, piece in zip(late, waiting):
        pieces[block] = passed_along(piece, "dom", -block_offset(block))
    place = lax.axis_index("dom")[None].astype(jnp.int32)
    density, own, mail = density_and_terms(
        place,
        e_high,
        e_low,
        branches,
        halo_request,
        flat_deriv,
        ready,
        [pieces[block] for block in range(block_count)],
    )
    arrived = lax.all_to_all(mail, "dom", 0, 0, tiled=True)
    forces = pl.pallas_call(
        collect,
        out_shape=jax.ShapeDtypeStruct((3, own.shape[1]), jnp.float32),
        in_specs=[
            pl.BlockSpec(memory_space=pltpu.SMEM),
            pl.BlockSpec(memory_space=pltpu.VMEM),
            pl.BlockSpec(memory_space=pltpu.VMEM),
        ],
        out_specs=pl.BlockSpec(memory_space=pltpu.VMEM),
    )(place, arrived, own)
    return (density, forces)


def solution(mesh):
    in_specs = (
        P("dom", None),
        P("dom", None, None, None),
        P("dom", None),
        P(None, "dom", None, None),
        P(),
        P(),
        P(),
    )
    out_specs = (P("dom", None), P(None, "dom"))
    return jax.shard_map(
        per_device, mesh=mesh, in_specs=in_specs, out_specs=out_specs, check_vma=False
    )
```

profile of v0, /device:TPU:0, one launch (start us, length us, event | category | flops | bytes accessed | tf_op | source)
XLA Modules:
  0.0 120.8 jit_solution(6740055948621874164)
XLA Ops:
  0.6 1.6 %slice_bitcast_fusion.7 = f32[80,640]{1,0:T(8,128)} fusion(f32[1,8,80,1280]{3,2,1,0:T(8,128)} %param.8), kind=kLoop, calls=%fused_computation.7 | loop fusion | bytes 409600 | tf_op jit(solution)/shard_map/squeeze | solution.py:425
  2.2 2.4 %collective-permute-start.6 = (f32[80,640]{1,0:T(8,128)}, f32[80,640]{1,0:T(8,128)S(1)}, u32[]{:S(2)}, u32[]{:S(2)}) collective-permute-start(f32[80,640]{1,0:T(8,128)} %slice_bitcast_fusion.7), channel_id=1, source_target_pairs={{0,3},{1,4},{2,5},{3,6},{4,7},{5,8},{6,9},{7,10},{8,11},{9,12},{10... | collective-permute-start | bytes 614408 | tf_op jit(solution)/shard_map/ppermute | solution.py:22
  4.6 2.6 %slice_bitcast_fusion = (f32[80,640]{1,0:T(8,128)}, f32[80,640]{1,0:T(8,128)}, f32[80,640]{1,0:T(8,128)}, f32[80,640]{1,0:T(8,128)}, f32[80,640]{1,0:T(8,128)}, /*index=5*/f32[80,640]{1,0:T(8,128)}, f32[80,640]{1,0:T(8,128)}) fusion(f32[1,8,80,1280]{3,2,1,0:T(8,128)} %param.8), kind=kLoop, calls=%fused_computation | loop fusion | bytes 2867200 | tf_op jit(solution)/shard_map/squeeze | solution.py:430
  7.2 1.5 %collective-permute-start.5 = (f32[80,640]{1,0:T(8,128)}, f32[80,640]{1,0:T(8,128)}, u32[]{:S(2)}, u32[]{:S(2)}) collective-permute-start(f32[80,640]{1,0:T(8,128)} %get-tuple-element.61), channel_id=1, source_target_pairs={{0,2},{1,3},{2,4},{3,5},{4,6},{5,7},{6,8},{7,9},{8,10},{9,11},{10,... | collective-permute-start | bytes 614408 | tf_op jit(solution)/shard_map/ppermute | solution.py:22
  8.7 3.6 %collective-permute-start.3 = (f32[80,640]{1,0:T(8,128)}, f32[80,640]{1,0:T(8,128)}, u32[]{:S(2)}, u32[]{:S(2)}) collective-permute-start(f32[80,640]{1,0:T(8,128)} %get-tuple-element.62), channel_id=1, source_target_pairs={{0,28},{1,29},{2,30},{3,31},{4,0},{5,1},{6,2},{7,3},{8,4},{9,5},{1... | collective-permute-start | bytes 614408 | tf_op jit(solution)/shard_map/ppermute | solution.py:22
  12.4 1.2 collective-permute-start.2
  13.5 2.3 %collective-permute-start.1 = (f32[80,640]{1,0:T(8,128)}, f32[80,640]{1,0:T(8,128)}, u32[]{:S(2)}, u32[]{:S(2)}) collective-permute-start(f32[80,640]{1,0:T(8,128)} %get-tuple-element.64), channel_id=1, source_target_pairs={{0,30},{1,31},{2,0},{3,1},{4,2},{5,3},{6,4},{7,5},{8,6},{9,7},{10,... | collective-permute-start | bytes 614408 | tf_op jit(solution)/shard_map/ppermute | solution.py:22
  17.2 7.1 %fusion = (f32[1,160,4,1280]{3,2,1,0:T(4,128)}, f32[1,160,4,1280]{3,2,1,0:T(4,128)}, f32[1,160,4,1280]{3,2,1,0:T(4,128)}) fusion(f32[3,160,4,1280]{3,2,1,0:T(4,128)} %param.10), kind=kLoop, calls=%fused_computation.8 | loop fusion | bytes 19660800 | tf_op jit(solution)/shard_map/slice | solution.py:432
  24.3 0.0 copy-start.2
  24.3 0.0 copy-start.3
  24.3 3.3 %reshape_squeeze.9.refs_0_ = f32[640,1280]{1,0:T(8,128)S(1)} reshape(f32[1,160,4,1280]{3,2,1,0:T(4,128)} %get-tuple-element.59) | data formatting | bytes 6553600 | tf_op jit(solution)/shard_map/reshape;squeeze | solution.py:432
  27.6 0.0 copy-done.2
  27.6 0.0 copy-done.3
  27.6 0.0 copy-start.1
  27.6 1.9 %copy-done.1 = f32[640,1280]{1,0:T(8,128)S(1)} copy-done((f32[640,1280]{1,0:T(8,128)S(1)}, f32[640,1280]{1,0:T(8,128)}, u32[]{:S(2)}) %copy-start.1) | copy-done | bytes 3276824
  29.6 7.4 %shard_map.86 = (bf16[640,640]{1,0:T(8,128)(2,1)S(1)}, bf16[640,640]{1,0:T(8,128)(2,1)S(1)}, f32[640,640]{1,0:T(8,128)S(1)}, f32[640,640]{1,0:T(8,128)S(1)}, f32...) custom-call(f32[1]{0:T(128)S(6)} %copy.10.high_end, ...), custom_call_target="tpu_custom_call" | custom-call | flops 4194304000 | bytes 13000000 | tf_op jit(solution)/shard_map/pallas_call | solution.py:363
  37.0 0.0 copy-start.4
  37.0 1.2 copy-done.4
  38.1 0.0 copy-start.6
  38.1 1.3 %copy-done.6 = f32[640,640]{1,0:T(8,128)} copy-done((f32[640,640]{1,0:T(8,128)}, f32[640,640]{1,0:T(8,128)S(1)}, u32[]{:S(2)}) %copy-start.6) | copy-done | bytes 1638424
  39.4 0.0 copy-start.8
  39.4 1.2 copy-done.8
  40.6 0.0 copy-start.10
  40.6 1.2 copy-done.10
  41.7 0.0 copy-start.12
  41.7 0.9 copy-done.12
  42.6 0.0 copy-start.14
  42.6 0.9 copy-done.14
  43.6 0.0 copy-start.16
  43.6 0.9 copy-done.16
  44.4 0.0 copy-start.18
  44.4 0.9 copy-done.18
  45.3 0.7 copy-done.20
  46.1 0.0 collective-permute-done.6.refs_19_
  46.1 1.1 collective-permute-start
  47.2 0.0 collective-permute-done.5.refs_18_
  47.2 0.0 collective-permute-start.4
  47.2 0.0 collective-permute-done.3.refs_16_
  47.2 0.9 collective-permute-start.7
  48.1 5.0 %reshape_squeeze.11.refs_2_ = f32[640,1280]{1,0:T(8,128)} reshape(f32[1,160,4,1280]{3,2,1,0:T(4,128)} %get-tuple-element.58) | data formatting | bytes 6553600 | tf_op jit(solution)/shard_map/reshape;squeeze | solution.py:432
  53.1 5.0 %reshape_squeeze.10.refs_1_ = f32[640,1280]{1,0:T(8,128)} reshape(f32[1,160,4,1280]{3,2,1,0:T(4,128)} %get-tuple-element.60) | data formatting | bytes 6553600 | tf_op jit(solution)/shard_map/reshape;squeeze | solution.py:432
  58.1 0.0 collective-permute-done.2.refs_15_
  58.1 0.0 collective-permute-done.1.refs_14_
  58.1 0.0 collective-permute-done.refs_13_
  58.1 1.1 collective-permute-done.4.refs_17_
  59.2 0.0 collective-permute-done.7.refs_20_
  59.2 0.0 copy-start.5
  59.2 1.4 %copy-done.5 = f32[640,640]{1,0:T(8,128)S(1)} copy-done((f32[640,640]{1,0:T(8,128)S(1)}, f32[640,640]{1,0:T(8,128)}, u32[]{:S(2)}) %copy-start.5) | copy-done | bytes 1638424
  60.6 0.0 copy-start.7
  60.6 1.4 %copy-done.7 = f32[640,640]{1,0:T(8,128)S(1)} copy-done((f32[640,640]{1,0:T(8,128)S(1)}, f32[640,640]{1,0:T(8,128)}, u32[]{:S(2)}) %copy-start.7) | copy-done | bytes 1638424
  62.1 0.0 copy-start.9
  62.1 1.4 %copy-done.9 = f32[640,640]{1,0:T(8,128)S(1)} copy-done((f32[640,640]{1,0:T(8,128)S(1)}, f32[640,640]{1,0:T(8,128)}, u32[]{:S(2)}) %copy-start.9) | copy-done | bytes 1638424
  63.5 0.0 copy-start.11
  63.5 1.4 %copy-done.11 = f32[640,640]{1,0:T(8,128)S(1)} copy-done((f32[640,640]{1,0:T(8,128)S(1)}, f32[640,640]{1,0:T(8,128)}, u32[]{:S(2)}) %copy-start.11) | copy-done | bytes 1638424
  64.9 1.1 copy-done.13
  66.1 1.1 copy-done.15
  67.2 1.1 copy-done.17
  68.4 1.1 copy-done.19
  69.5 1.0 copy-done.21
  70.5 37.0 %shard_map.87 = (f32[640,1280]{1,0:T(8,128)}, f32[8,160]{1,0:T(8,128)S(1)}, f32[32,4,128]{2,1,0:T(4,128)S(1)}) custom-call(s32[1]{0:T(128)} %bitcast.place, f32[1]{0:T(128)S(6)} %copy.10.high_end, f32[1]{0:T(128)S(6)} %copy.9.low_end, s32[5]{0:T(128)S(1)} %copy-done.3, s32[1,160]{1,0:T(1,128)S(1)} %copy-done.2, f32[640,1280]{1,0:T(8,128)S(1)} %reshape_squeeze.9.refs_0_, ...), custom_call_target="tpu_custom_call" | custom-call | flops 37748736000 | bytes 24000000 | tf_op jit(solution)/shard_map/pallas_call | solution.py:388
  107.6 0.0 copy-start
  107.6 11.4 %all_to_all.5.mail = f32[32,4,128]{2,1,0:T(4,128)} all-to-all(f32[32,4,128]{2,1,0:T(4,128)S(1)} %get-tuple-element.56), channel_id=1, replica_groups=mesh['dom'=32] {'dom'}, dimensions={0} | all-to-all | bytes 131072 | tf_op jit(solution)/shard_map/all_to_all | solution.py:449
  119.0 0.0 copy-done
  119.0 1.8 %shard_map.88 = f32[3,160]{1,0:T(4,128)} custom-call(s32[1]{0:T(128)} %bitcast.place, f32[32,4,128]{2,1,0:T(4,128)} %all_to_all.5.mail, f32[8,160]{1,0:T(8,128)} %copy-done), custom_call_target="tpu_custom_call" | custom-call | tf_op jit(solution)/shard_map/pallas_call | solution.py:450
  (6 shorter events, 0.0 us)
Async XLA Ops:
  2.2 43.8 %collective-permute-start.6 = (f32[80,640]{1,0:T(8,128)}, f32[80,640]{1,0:T(8,128)S(1)}, u32[]{:S(2)}, u32[]{:S(2)}) collective-permute-start(f32[80,640]{1,0:T(8,128)} %slice_bitcast_fusion.7), channel_id=1, source_target_pairs={{0,3},{1,4},{2,5},{3,6},{4,7},{5,8},{6,9},{7,10},{8,11},{9,12},{10... | collective-permute-start | bytes 614408 | tf_op jit(solution)/shard_map/ppermute | solution.py:22
  7.2 40.0 %collective-permute-start.5 = (f32[80,640]{1,0:T(8,128)}, f32[80,640]{1,0:T(8,128)}, u32[]{:S(2)}, u32[]{:S(2)}) collective-permute-start(f32[80,640]{1,0:T(8,128)} %get-tuple-element.61), channel_id=1, source_target_pairs={{0,2},{1,3},{2,4},{3,5},{4,6},{5,7},{6,8},{7,9},{8,10},{9,11},{10,... | collective-permute-start | bytes 614408 | tf_op jit(solution)/shard_map/ppermute | solution.py:22
  8.7 38.5 %collective-permute-start.3 = (f32[80,640]{1,0:T(8,128)}, f32[80,640]{1,0:T(8,128)}, u32[]{:S(2)}, u32[]{:S(2)}) collective-permute-start(f32[80,640]{1,0:T(8,128)} %get-tuple-element.62), channel_id=1, source_target_pairs={{0,28},{1,29},{2,30},{3,31},{4,0},{5,1},{6,2},{7,3},{8,4},{9,5},{1... | collective-permute-start | bytes 614408 | tf_op jit(solution)/shard_map/ppermute | solution.py:22
  12.4 45.8 %collective-permute-start.2 = (f32[80,640]{1,0:T(8,128)}, f32[80,640]{1,0:T(8,128)}, u32[]{:S(2)}, u32[]{:S(2)}) collective-permute-start(f32[80,640]{1,0:T(8,128)} %get-tuple-element.63), channel_id=1, source_target_pairs={{0,29},{1,30},{2,31},{3,0},{4,1},{5,2},{6,3},{7,4},{8,5},{9,6},{10... | collective-permute-start | bytes 614408 | tf_op jit(solution)/shard_map/ppermute | solution.py:22
  13.5 44.6 %collective-permute-start.1 = (f32[80,640]{1,0:T(8,128)}, f32[80,640]{1,0:T(8,128)}, u32[]{:S(2)}, u32[]{:S(2)}) collective-permute-start(f32[80,640]{1,0:T(8,128)} %get-tuple-element.64), channel_id=1, source_target_pairs={{0,30},{1,31},{2,0},{3,1},{4,2},{5,3},{6,4},{7,5},{8,6},{9,7},{10,... | collective-permute-start | bytes 614408 | tf_op jit(solution)/shard_map/ppermute | solution.py:22
  24.3 3.3 %copy-start.2 = (s32[1,160]{1,0:T(1,128)S(1)}, s32[1,160]{1,0:T(1,128)}, u32[]{:S(2)}) copy-start(s32[1,160]{1,0:T(1,128)} %request.3) | copy-start | bytes 1924
  24.3 3.3 %copy-start.3 = (s32[5]{0:T(128)S(1)}, s32[5]{0:T(128)}, u32[]{:S(2)}) copy-start(s32[5]{0:T(128)} %branches.3) | copy-start | bytes 64
  27.6 1.9 %copy-start.1 = (f32[640,1280]{1,0:T(8,128)S(1)}, f32[640,1280]{1,0:T(8,128)}, u32[]{:S(2)}) copy-start(f32[640,1280]{1,0:T(8,128)} %core.1) | copy-start | bytes 9830404
  37.0 1.2 copy-start.4
  38.1 1.3 %copy-start.6 = (f32[640,640]{1,0:T(8,128)}, f32[640,640]{1,0:T(8,128)S(1)}, u32[]{:S(2)}) copy-start(f32[640,640]{1,0:T(8,128)S(1)} %get-tuple-element.45.refs_6_) | copy-start | bytes 4915204
  39.4 1.2 copy-start.8
  40.6 1.2 copy-start.10
  41.7 0.9 copy-start.12
  42.6 0.9 copy-start.14
  43.6 0.9 copy-start.16
  44.4 0.9 copy-start.18
  45.3 0.7 copy-start.20
  46.1 12.0 %collective-permute-start = (f32[80,640]{1,0:T(8,128)}, f32[80,640]{1,0:T(8,128)}, u32[]{:S(2)}, u32[]{:S(2)}) collective-permute-start(f32[80,640]{1,0:T(8,128)} %get-tuple-element.52), channel_id=1, source_target_pairs={{0,31},{1,0},{2,1},{3,2},{4,3},{5,4},{6,5},{7,6},{8,7},{9,8},{10,9... | collective-permute-start | bytes 614408 | tf_op jit(solution)/shard_map/ppermute | solution.py:22
  47.2 12.0 %collective-permute-start.4 = (f32[80,640]{1,0:T(8,128)}, f32[80,640]{1,0:T(8,128)}, u32[]{:S(2)}, u32[]{:S(2)}) collective-permute-start(f32[80,640]{1,0:T(8,128)} %get-tuple-element.53), channel_id=1, source_target_pairs={{0,1},{1,2},{2,3},{3,4},{4,5},{5,6},{6,7},{7,8},{8,9},{9,10},{10,1... | collective-permute-start | bytes 614408 | tf_op jit(solution)/shard_map/ppermute | solution.py:22
  47.2 12.0 %collective-permute-start.7 = (f32[80,640]{1,0:T(8,128)}, f32[80,640]{1,0:T(8,128)}, u32[]{:S(2)}, u32[]{:S(2)}) collective-permute-start(f32[80,640]{1,0:T(8,128)} %get-tuple-element.54), channel_id=1, source_target_pairs={{0,4},{1,5},{2,6},{3,7},{4,8},{5,9},{6,10},{7,11},{8,12},{9,13},{1... | collective-permute-start | bytes 614408 | tf_op jit(solution)/shard_map/ppermute | solution.py:22
  59.2 1.4 %copy-start.5 = (f32[640,640]{1,0:T(8,128)S(1)}, f32[640,640]{1,0:T(8,128)}, u32[]{:S(2)}) copy-start(f32[640,640]{1,0:T(8,128)} %copy-done.4) | copy-start | bytes 4915204
  60.6 1.4 %copy-start.7 = (f32[640,640]{1,0:T(8,128)S(1)}, f32[640,640]{1,0:T(8,128)}, u32[]{:S(2)}) copy-start(f32[640,640]{1,0:T(8,128)} %copy-done.6) | copy-start | bytes 4915204
  62.1 1.4 %copy-start.9 = (f32[640,640]{1,0:T(8,128)S(1)}, f32[640,640]{1,0:T(8,128)}, u32[]{:S(2)}) copy-start(f32[640,640]{1,0:T(8,128)} %copy-done.8) | copy-start | bytes 4915204
  63.5 1.4 %copy-start.11 = (f32[640,640]{1,0:T(8,128)S(1)}, f32[640,640]{1,0:T(8,128)}, u32[]{:S(2)}) copy-start(f32[640,640]{1,0:T(8,128)} %copy-done.10) | copy-start | bytes 4915204
  64.9 1.1 copy-start.13
  66.1 1.1 copy-start.15
  67.2 1.1 copy-start.17
  68.4 1.1 copy-start.19
  69.5 1.0 copy-start.21
  107.6 11.4 %copy-start = (f32[8,160]{1,0:T(8,128)}, f32[8,160]{1,0:T(8,128)S(1)}, u32[]{:S(2)}) copy-start(f32[8,160]{1,0:T(8,128)S(1)} %get-tuple-element.57.own) | copy-start | bytes 15364
where the time goes:
time: 122 us; the launch traced here: 121 us
  local copies, waits for them, and re-layouts  46.9 us (38%)
  Pallas kernels  46.3 us (38%)
  starting transfers between devices  13 us (11%)
  blocking collectives  11.4 us (9%)
  between operations  2.02 us (2%)
    pallas_call x1, Pallas kernels, density_and_terms(): pl.pallas_call(kernel, out_shape=[jax.ShapeDtypeStruct((rows, order), jnp...  37 us
    unnamed x44, local copies, waits for them, and re-layouts  22.3 us
    another operation x3, local copies, waits for them, and re-layouts, per_device(): flat_deriv = [deriv[c].reshape(row_count, order_all) for c in range(3)]  13.3 us
    ppermute x8, starting transfers between devices, passed_along(): return lax.ppermute(value, axis, pairs)  13 us
    all_to_all x1, blocking collectives, per_device(): arrived = lax.all_to_all(mail, 'dom', 0, 0, tiled=True)  11.4 us
    pallas_call x1, Pallas kernels, own_part(): pl.pallas_call(own_kernel, out_shape=[jax.ShapeDtypeStruct(*kind) for kin...  7.41 us
    slice x1, local copies, waits for them, and re-layouts, per_device(): flat_deriv = [deriv[c].reshape(row_count, order_all) for c in range(3)]  7.09 us
    squeeze x1, local copies, waits for them, and re-layouts, per_device(): pieces[block] = passed_along(halo[block], 'dom', -block_offset(block))  2.6 us
  transfers between devices with their start and end apart: 8, of which 1 were waited for; matrix products, arithmetic and copies ran while one was open for 19% of the time, Pallas kernels for 6%

commit v1 on v0

--- a/solution.py
+++ b/solution.py
@@ -184,8 +184,7 @@
                 store_matrix(value, later, row, col)
 
 
-def kernel(place, high_end, low_end, branches, request, *refs):
-    deriv, refs = refs[:3], refs[3:]
+def kernel(place, high_end, low_end, branches, request, deriv, *refs):
     block_count = 2 * NB
     (high_cross, low_cross, x_cross, y_cross, y_halo, x_own, high_own, low_own, own_col, own_row) = refs[:10]
     pieces = refs[10 : 10 + block_count]
@@ -201,7 +200,7 @@
     left, right = slice(0, rows), slice(rows, order)
 
     deriv_copies = [
-        pltpu.make_async_copy(deriv[c], deriv_held.at[c], deriv_sems.at[c]) for c in range(3)
+        pltpu.make_async_copy(deriv.at[c], deriv_held.at[c], deriv_sems.at[c]) for c in range(3)
     ]
     for copy in deriv_copies:
         copy.start()
@@ -379,7 +378,7 @@
 
 
 def density_and_terms(place, high_end, low_end, branches, request, deriv, ready, pieces):
-    rows, order = deriv[0].shape
+    rows, order = deriv.shape[1:]
     atoms = rows // ORB
     vmem = pl.BlockSpec(memory_space=pltpu.VMEM)
     smem = pl.BlockSpec(memory_space=pltpu.SMEM)
@@ -392,7 +391,7 @@
             jax.ShapeDtypeStruct((8, atoms), jnp.float32),
             jax.ShapeDtypeStruct((lax.axis_size("dom"), 4, SUB), jnp.float32),
         ],
-        in_specs=[smem, smem, smem, smem, vmem] + [anywhere] * 3 + [vmem] * (len(ready) + len(pieces)),
+        in_specs=[smem, smem, smem, smem, vmem, anywhere] + [vmem] * (len(ready) + len(pieces)),
         out_specs=[anywhere, vmem, vmem],
         scratch_shapes=[
             pltpu.VMEM(square, jnp.float32),
@@ -414,7 +413,7 @@
         cost_estimate=pl.CostEstimate(
             flops=2 * 3 * 3 * order**3, bytes_accessed=24_000_000, transcendentals=0
         ),
-    )(place, high_end, low_end, branches, request, *deriv, *ready, *pieces)
+    )(place, high_end, low_end, branches, request, deriv, *ready, *pieces)
 
 
 def per_device(ham_core, halo_rows, halo_request, deriv, e_low, e_high, branches):
@@ -428,11 +427,8 @@
     halo = rest[0, :, :, row_count:]
     for block in early[1:]:
         pieces[block] = passed_along(halo[block], "dom", -block_offset(block))
-    ready = own_part(e_high, e_low, branches, ham_core, halo_request)
-    flat_deriv = [deriv[c].reshape(row_count, order_all) for c in range(3)]
-    waiting, ready, flat_deriv[0] = lax.optimization_barrier(
-        ([halo[block] for block in late], ready, flat_deriv[0])
-    )
+    *ready, own_row = own_part(e_high, e_low, branches, ham_core, halo_request)
+    waiting, own_row = lax.optimization_barrier(([halo[block] for block in late], own_row))
     for block, piece in zip(late, waiting):
         pieces[block] = passed_along(piece, "dom", -block_offset(block))
     place = lax.axis_index("dom")[None].astype(jnp.int32)
@@ -442,8 +438,8 @@
         e_low,
         branches,
         halo_request,
-        flat_deriv,
-        ready,
+        deriv.reshape(3, row_count, order_all),
+        [*ready, own_row],
         [pieces[block] for block in range(block_count)],
     )
     arrived = lax.all_to_all(mail, "dom", 0, 0, tiled=True)

time: 122 us -> 107 us (0.88)
  local copies, waits for them, and re-layouts: 46.9 us -> 33.5 us
    another operation x3 -> x0, local copies, waits for them, and re-layouts: 13.3 us -> none  [per_device(): flat_deriv = [deriv[c].reshape(row_count, order_all) for c in range(3)]]
    reshape x0 -> x1, local copies, waits for them, and re-layouts: none -> 12.2 us  [per_device(): deriv.reshape(3, row_count, order_all)]
    slice x1 -> x0, local copies, waits for them, and re-layouts: 7.09 us -> none  [per_device(): flat_deriv = [deriv[c].reshape(row_count, order_all) for c in range(3)]]
    unnamed x44 -> x40, local copies, waits for them, and re-layouts: 22.3 us -> 17.8 us
  transfers between devices with their start and end apart: 8 -> 8, of which waited for: 1 -> 0; matrix products, arithmetic and copies ran while one was open for 19% -> 14% of each run, Pallas kernels for 6% -> 7%
where the time goes in v1:
time: 107 us; the launch traced here: 106 us
  Pallas kernels  45.2 us (42%)
  local copies, waits for them, and re-layouts  33.5 us (31%)
  starting transfers between devices  13.1 us (12%)
  blocking collectives  12.5 us (12%)
  between operations  2.06 us (2%)
    pallas_call x1, Pallas kernels, density_and_terms(): pl.pallas_call(kernel, out_shape=[jax.ShapeDtypeStruct((rows, order), jnp...  36.1 us
    unnamed x40, local copies, waits for them, and re-layouts  17.8 us
    ppermute x8, starting transfers between devices, passed_along(): return lax.ppermute(value, axis, pairs)  13.1 us
    all_to_all x1, blocking collectives, per_device(): arrived = lax.all_to_all(mail, 'dom', 0, 0, tiled=True)  12.5 us
    reshape x1, local copies, waits for them, and re-layouts, per_device(): deriv.reshape(3, row_count, order_all)  12.2 us
    pallas_call x1, Pallas kernels, own_part(): pl.pallas_call(own_kernel, out_shape=[jax.ShapeDtypeStruct(*kind) for kin...  7.25 us
    squeeze x1, local copies, waits for them, and re-layouts, per_device(): pieces[block] = passed_along(halo[block], 'dom', -block_offset(block))  2.34 us
  transfers between devices with their start and end apart: 8, of which 0 were waited for; matrix products, arithmetic and copies ran while one was open for 14% of the time, Pallas kernels for 7%

profile of v1, /device:TPU:0, one launch (start us, length us, event | category | flops | bytes accessed | tf_op | source)
XLA Modules:
  0.0 106.3 jit_solution(15976965919767311374)
XLA Ops:
  0.6 0.0 copy-start.3
  0.6 0.0 copy-start.2
  0.6 0.0 copy-start.1
  0.7 1.1 %slice_bitcast_fusion.7 = f32[80,640]{1,0:T(8,128)S(1)} fusion(f32[1,8,80,1280]{3,2,1,0:T(8,128)} %param.8), kind=kLoop, calls=%fused_computation.7 | loop fusion | bytes 409600 | tf_op jit(solution)/shard_map/squeeze | solution.py:424
  1.8 2.4 %collective-permute-start.6 = (f32[80,640]{1,0:T(8,128)S(1)}, f32[80,640]{1,0:T(8,128)S(1)}, u32[]{:S(2)}, u32[]{:S(2)}) collective-permute-start(f32[80,640]{1,0:T(8,128)S(1)} %slice_bitcast_fusion.7), channel_id=1, source_target_pairs={{0,3},{1,4},{2,5},{3,6},{4,7},{5,8},{6,9},{7,10},{8,11},{9,12},{10... | collective-permute-start | bytes 614408 | tf_op jit(solution)/shard_map/ppermute | solution.py:22
  4.2 2.3 %slice_bitcast_fusion = (f32[80,640]{1,0:T(8,128)S(1)}, f32[80,640]{1,0:T(8,128)S(1)}, f32[80,640]{1,0:T(8,128)}, f32[80,640]{1,0:T(8,128)}, f32[80,640]{1,0:T(8...) fusion(f32[1,8,80,1280]{3,2,1,0:T(8,128)} %param.8), kind=kLoop, calls=%fused_computation | loop fusion | bytes 2867200 | tf_op jit(solution)/shard_map/squeeze | solution.py:429
  6.5 1.5 %collective-permute-start.5 = (f32[80,640]{1,0:T(8,128)S(1)}, f32[80,640]{1,0:T(8,128)S(1)}, u32[]{:S(2)}, u32[]{:S(2)}) collective-permute-start(f32[80,640]{1,0:T(8,128)S(1)} %get-tuple-element.38), channel_id=1, source_target_pairs={{0,2},{1,3},{2,4},{3,5},{4,6},{5,7},{6,8},{7,9},{8,10},{9,11},{10,... | collective-permute-start | bytes 614408 | tf_op jit(solution)/shard_map/ppermute | solution.py:22
  8.0 3.6 %collective-permute-start.3 = (f32[80,640]{1,0:T(8,128)S(1)}, f32[80,640]{1,0:T(8,128)S(1)}, u32[]{:S(2)}, u32[]{:S(2)}) collective-permute-start(f32[80,640]{1,0:T(8,128)S(1)} %get-tuple-element.39), channel_id=1, source_target_pairs={{0,28},{1,29},{2,30},{3,31},{4,0},{5,1},{6,2},{7,3},{8,4},{9,5},{1... | collective-permute-start | bytes 614408 | tf_op jit(solution)/shard_map/ppermute | solution.py:22
  11.7 1.2 %collective-permute-start.2 = (f32[80,640]{1,0:T(8,128)}, f32[80,640]{1,0:T(8,128)S(1)}, u32[]{:S(2)}, u32[]{:S(2)}) collective-permute-start(f32[80,640]{1,0:T(8,128)} %get-tuple-element.40), channel_id=1, source_target_pairs={{0,29},{1,30},{2,31},{3,0},{4,1},{5,2},{6,3},{7,4},{8,5},{9,6},{10... | collective-permute-start | bytes 614408 | tf_op jit(solution)/shard_map/ppermute | solution.py:22
  12.8 2.3 %collective-permute-start.1 = (f32[80,640]{1,0:T(8,128)}, f32[80,640]{1,0:T(8,128)S(1)}, u32[]{:S(2)}, u32[]{:S(2)}) collective-permute-start(f32[80,640]{1,0:T(8,128)} %get-tuple-element.41), channel_id=1, source_target_pairs={{0,30},{1,31},{2,0},{3,1},{4,2},{5,3},{6,4},{7,5},{8,6},{9,7},{10,... | collective-permute-start | bytes 614408 | tf_op jit(solution)/shard_map/ppermute | solution.py:22
  16.5 0.0 copy-done.3
  16.5 0.0 copy-done.2
  16.5 0.0 copy-done.1
  16.5 7.3 %shard_map.86 = (bf16[640,640]{1,0:T(8,128)(2,1)S(1)}, bf16[640,640]{1,0:T(8,128)(2,1)S(1)}, f32[640,640]{1,0:T(8,128)S(1)}, f32[640,640]{1,0:T(8,128)S(1)}, f32...) custom-call(f32[1]{0:T(128)S(6)} %copy.10.high_end, ...), custom_call_target="tpu_custom_call" | custom-call | flops 4194304000 | bytes 13000000 | tf_op jit(solution)/shard_map/pallas_call | solution.py:362
  23.8 0.0 copy-start.4
  23.8 1.2 %copy-done.4 = f32[640,640]{1,0:T(8,128)} copy-done((f32[640,640]{1,0:T(8,128)}, f32[640,640]{1,0:T(8,128)S(1)}, u32[]{:S(2)}) %copy-start.4) | copy-done | bytes 1638424
  24.9 0.0 copy-start.6
  24.9 1.2 %copy-done.6 = f32[640,640]{1,0:T(8,128)} copy-done((f32[640,640]{1,0:T(8,128)}, f32[640,640]{1,0:T(8,128)S(1)}, u32[]{:S(2)}) %copy-start.6) | copy-done | bytes 1638424
  26.1 0.0 copy-start.8
  26.1 1.3 %copy-done.8 = f32[640,640]{1,0:T(8,128)} copy-done((f32[640,640]{1,0:T(8,128)}, f32[640,640]{1,0:T(8,128)S(1)}, u32[]{:S(2)}) %copy-start.8) | copy-done | bytes 1638424
  27.4 0.0 copy-start.10
  27.4 0.9 copy-done.10
  28.3 0.0 copy-start.12
  28.3 0.9 copy-done.12
  29.2 0.0 copy-start.14
  29.2 0.9 copy-done.14
  30.1 0.0 copy-start.16
  30.1 0.9 copy-done.16
  31.0 0.0 copy-start.18
  31.0 0.7 copy-done.18
  31.7 0.0 collective-permute-done.6.refs_16_
  31.7 1.1 %collective-permute-start = (f32[80,640]{1,0:T(8,128)}, f32[80,640]{1,0:T(8,128)S(1)}, u32[]{:S(2)}, u32[]{:S(2)}) collective-permute-start(f32[80,640]{1,0:T(8,128)} %get-tuple-element.32), channel_id=1, source_target_pairs={{0,31},{1,0},{2,1},{3,2},{4,3},{5,4},{6,5},{7,6},{8,7},{9,8},{10,9... | collective-permute-start | bytes 614408 | tf_op jit(solution)/shard_map/ppermute | solution.py:22
  32.9 0.0 collective-permute-done.5.refs_15_
  32.9 0.0 collective-permute-start.4
  32.9 0.0 collective-permute-done.3.refs_13_
  32.9 0.9 collective-permute-start.7
  33.7 12.2 %reshape.21.deriv = f32[3,640,1280]{2,1,0:T(8,128)} reshape(f32[3,160,4,1280]{3,2,1,0:T(4,128)} %param.10) | data formatting | bytes 19660800 | tf_op jit(solution)/shard_map/reshape | solution.py:441
  46.0 0.0 collective-permute-done.2.refs_12_
  46.0 0.0 collective-permute-done.1.refs_11_
  46.0 0.0 collective-permute-done.refs_10_
  46.0 0.0 collective-permute-done.4.refs_14_
  46.0 0.0 collective-permute-done.7.refs_17_
  46.0 0.0 copy-start.5
  46.0 1.4 %copy-done.5 = f32[640,640]{1,0:T(8,128)S(1)} copy-done((f32[640,640]{1,0:T(8,128)S(1)}, f32[640,640]{1,0:T(8,128)}, u32[]{:S(2)}) %copy-start.5) | copy-done | bytes 1638424
  47.5 0.0 copy-start.7
  47.5 1.4 %copy-done.7 = f32[640,640]{1,0:T(8,128)S(1)} copy-done((f32[640,640]{1,0:T(8,128)S(1)}, f32[640,640]{1,0:T(8,128)}, u32[]{:S(2)}) %copy-start.7) | copy-done | bytes 1638424
  48.9 0.0 copy-start.9
  48.9 1.4 %copy-done.9 = f32[640,640]{1,0:T(8,128)S(1)} copy-done((f32[640,640]{1,0:T(8,128)S(1)}, f32[640,640]{1,0:T(8,128)}, u32[]{:S(2)}) %copy-start.9) | copy-done | bytes 1638424
  50.3 0.0 copy-start.11
  50.3 1.1 %copy-done.11 = bf16[640,640]{1,0:T(8,128)(2,1)S(1)} copy-done((bf16[640,640]{1,0:T(8,128)(2,1)S(1)}, bf16[640,640]{1,0:T(8,128)(2,1)}, u32[]{:S(2)}) %copy-start.11) | copy-done | bytes 819224
  51.5 0.0 copy-start.13
  51.5 1.1 %copy-done.13 = bf16[640,640]{1,0:T(8,128)(2,1)S(1)} copy-done((bf16[640,640]{1,0:T(8,128)(2,1)S(1)}, bf16[640,640]{1,0:T(8,128)(2,1)}, u32[]{:S(2)}) %copy-start.13) | copy-done | bytes 819224
  52.6 0.0 copy-start.15
  52.6 1.1 %copy-done.15 = bf16[640,640]{1,0:T(8,128)(2,1)S(1)} copy-done((bf16[640,640]{1,0:T(8,128)(2,1)S(1)}, bf16[640,640]{1,0:T(8,128)(2,1)}, u32[]{:S(2)}) %copy-start.15) | copy-done | bytes 819224
  53.8 0.0 copy-start.17
  53.8 1.1 %copy-done.17 = bf16[640,640]{1,0:T(8,128)(2,1)S(1)} copy-done((bf16[640,640]{1,0:T(8,128)(2,1)S(1)}, bf16[640,640]{1,0:T(8,128)(2,1)}, u32[]{:S(2)}) %copy-start.17) | copy-done | bytes 819224
  54.9 0.0 copy-start.19
  54.9 1.0 copy-done.19
  55.9 36.1 %shard_map.87 = (f32[640,1280]{1,0:T(8,128)}, f32[8,160]{1,0:T(8,128)S(1)}, f32[32,4,128]{2,1,0:T(4,128)S(1)}) custom-call(s32[1]{0:T(128)} %bitcast.place, f32[1]{0:T(128)S(6)} %copy.10.high_end, f32[1]{0:T(128)S(6)} %copy.9.low_end, s32[5]{0:T(128)S(1)} %copy-done.3, s32[1,160]{1,0:T(1,128)S(1)} %copy-done.2, f32[3,640,1280]{2,1,0:T(8,128)} %reshape.21.deriv, ...), custom_call_target="tpu_custom_call" | custom-call | flops 37748736000 | bytes 24000000 | tf_op jit(solution)/shard_map/pallas_call | solution.py:387
  92.0 0.0 copy-start
  92.0 12.5 %all_to_all.5.mail = f32[32,4,128]{2,1,0:T(4,128)} all-to-all(f32[32,4,128]{2,1,0:T(4,128)S(1)} %get-tuple-element.36), channel_id=1, replica_groups=mesh['dom'=32] {'dom'}, dimensions={0} | all-to-all | bytes 131072 | tf_op jit(solution)/shard_map/all_to_all | solution.py:445
  104.5 0.0 copy-done
  104.5 1.8 %shard_map.88 = f32[3,160]{1,0:T(4,128)} custom-call(s32[1]{0:T(128)} %bitcast.place, f32[32,4,128]{2,1,0:T(4,128)} %all_to_all.5.mail, f32[8,160]{1,0:T(8,128)} %copy-done), custom_call_target="tpu_custom_call" | custom-call | tf_op jit(solution)/shard_map/pallas_call | solution.py:446
Async XLA Ops:
  0.6 15.9 %copy-start.3 = (s32[5]{0:T(128)S(1)}, s32[5]{0:T(128)}, u32[]{:S(2)}) copy-start(s32[5]{0:T(128)} %branches.3) | copy-start | bytes 64
  0.6 15.9 %copy-start.2 = (s32[1,160]{1,0:T(1,128)S(1)}, s32[1,160]{1,0:T(1,128)}, u32[]{:S(2)}) copy-start(s32[1,160]{1,0:T(1,128)} %request.3) | copy-start | bytes 1924
  0.6 15.9 %copy-start.1 = (f32[640,1280]{1,0:T(8,128)S(1)}, f32[640,1280]{1,0:T(8,128)}, u32[]{:S(2)}) copy-start(f32[640,1280]{1,0:T(8,128)} %core.1) | copy-start | bytes 9830404
  1.8 30.0 %collective-permute-start.6 = (f32[80,640]{1,0:T(8,128)S(1)}, f32[80,640]{1,0:T(8,128)S(1)}, u32[]{:S(2)}, u32[]{:S(2)}) collective-permute-start(f32[80,640]{1,0:T(8,128)S(1)} %slice_bitcast_fusion.7), channel_id=1, source_target_pairs={{0,3},{1,4},{2,5},{3,6},{4,7},{5,8},{6,9},{7,10},{8,11},{9,12},{10... | collective-permute-start | bytes 614408 | tf_op jit(solution)/shard_map/ppermute | solution.py:22
  6.5 26.3 %collective-permute-start.5 = (f32[80,640]{1,0:T(8,128)S(1)}, f32[80,640]{1,0:T(8,128)S(1)}, u32[]{:S(2)}, u32[]{:S(2)}) collective-permute-start(f32[80,640]{1,0:T(8,128)S(1)} %get-tuple-element.38), channel_id=1, source_target_pairs={{0,2},{1,3},{2,4},{3,5},{4,6},{5,7},{6,8},{7,9},{8,10},{9,11},{10,... | collective-permute-start | bytes 614408 | tf_op jit(solution)/shard_map/ppermute | solution.py:22
  8.0 24.9 %collective-permute-start.3 = (f32[80,640]{1,0:T(8,128)S(1)}, f32[80,640]{1,0:T(8,128)S(1)}, u32[]{:S(2)}, u32[]{:S(2)}) collective-permute-start(f32[80,640]{1,0:T(8,128)S(1)} %get-tuple-element.39), channel_id=1, source_target_pairs={{0,28},{1,29},{2,30},{3,31},{4,0},{5,1},{6,2},{7,3},{8,4},{9,5},{1... | collective-permute-start | bytes 614408 | tf_op jit(solution)/shard_map/ppermute | solution.py:22
  11.7 34.3 %collective-permute-start.2 = (f32[80,640]{1,0:T(8,128)}, f32[80,640]{1,0:T(8,128)S(1)}, u32[]{:S(2)}, u32[]{:S(2)}) collective-permute-start(f32[80,640]{1,0:T(8,128)} %get-tuple-element.40), channel_id=1, source_target_pairs={{0,29},{1,30},{2,31},{3,0},{4,1},{5,2},{6,3},{7,4},{8,5},{9,6},{10... | collective-permute-start | bytes 614408 | tf_op jit(solution)/shard_map/ppermute | solution.py:22
  12.8 33.1 %collective-permute-start.1 = (f32[80,640]{1,0:T(8,128)}, f32[80,640]{1,0:T(8,128)S(1)}, u32[]{:S(2)}, u32[]{:S(2)}) collective-permute-start(f32[80,640]{1,0:T(8,128)} %get-tuple-element.41), channel_id=1, source_target_pairs={{0,30},{1,31},{2,0},{3,1},{4,2},{5,3},{6,4},{7,5},{8,6},{9,7},{10,... | collective-permute-start | bytes 614408 | tf_op jit(solution)/shard_map/ppermute | solution.py:22
  23.8 1.2 %copy-start.4 = (f32[640,640]{1,0:T(8,128)}, f32[640,640]{1,0:T(8,128)S(1)}, u32[]{:S(2)}) copy-start(f32[640,640]{1,0:T(8,128)S(1)} %get-tuple-element.23.refs_3_) | copy-start | bytes 4915204
  24.9 1.2 %copy-start.6 = (f32[640,640]{1,0:T(8,128)}, f32[640,640]{1,0:T(8,128)S(1)}, u32[]{:S(2)}) copy-start(f32[640,640]{1,0:T(8,128)S(1)} %get-tuple-element.24.refs_4_) | copy-start | bytes 4915204
  26.1 1.3 %copy-start.8 = (f32[640,640]{1,0:T(8,128)}, f32[640,640]{1,0:T(8,128)S(1)}, u32[]{:S(2)}) copy-start(f32[640,640]{1,0:T(8,128)S(1)} %get-tuple-element.25.refs_5_) | copy-start | bytes 4915204
  27.4 0.9 copy-start.10
  28.3 0.9 copy-start.12
  29.2 0.9 copy-start.14
  30.1 0.9 copy-start.16
  31.0 0.7 copy-start.18
  31.7 14.3 %collective-permute-start = (f32[80,640]{1,0:T(8,128)}, f32[80,640]{1,0:T(8,128)S(1)}, u32[]{:S(2)}, u32[]{:S(2)}) collective-permute-start(f32[80,640]{1,0:T(8,128)} %get-tuple-element.32), channel_id=1, source_target_pairs={{0,31},{1,0},{2,1},{3,2},{4,3},{5,4},{6,5},{7,6},{8,7},{9,8},{10,9... | collective-permute-start | bytes 614408 | tf_op jit(solution)/shard_map/ppermute | solution.py:22
  32.9 13.1 %collective-permute-start.4 = (f32[80,640]{1,0:T(8,128)}, f32[80,640]{1,0:T(8,128)S(1)}, u32[]{:S(2)}, u32[]{:S(2)}) collective-permute-start(f32[80,640]{1,0:T(8,128)} %get-tuple-element.33), channel_id=1, source_target_pairs={{0,1},{1,2},{2,3},{3,4},{4,5},{5,6},{6,7},{7,8},{8,9},{9,10},{10,1... | collective-permute-start | bytes 614408 | tf_op jit(solution)/shard_map/ppermute | solution.py:22
  32.9 13.1 %collective-permute-start.7 = (f32[80,640]{1,0:T(8,128)S(1)}, f32[80,640]{1,0:T(8,128)S(1)}, u32[]{:S(2)}, u32[]{:S(2)}) collective-permute-start(f32[80,640]{1,0:T(8,128)S(1)} %get-tuple-element.34), channel_id=1, source_target_pairs={{0,4},{1,5},{2,6},{3,7},{4,8},{5,9},{6,10},{7,11},{8,12},{9,13},{1... | collective-permute-start | bytes 614408 | tf_op jit(solution)/shard_map/ppermute | solution.py:22
  46.0 1.4 %copy-start.5 = (f32[640,640]{1,0:T(8,128)S(1)}, f32[640,640]{1,0:T(8,128)}, u32[]{:S(2)}) copy-start(f32[640,640]{1,0:T(8,128)} %copy-done.4) | copy-start | bytes 4915204
  47.5 1.4 %copy-start.7 = (f32[640,640]{1,0:T(8,128)S(1)}, f32[640,640]{1,0:T(8,128)}, u32[]{:S(2)}) copy-start(f32[640,640]{1,0:T(8,128)} %copy-done.6) | copy-start | bytes 4915204
  48.9 1.4 %copy-start.9 = (f32[640,640]{1,0:T(8,128)S(1)}, f32[640,640]{1,0:T(8,128)}, u32[]{:S(2)}) copy-start(f32[640,640]{1,0:T(8,128)} %copy-done.8) | copy-start | bytes 4915204
  50.3 1.1 %copy-start.11 = (bf16[640,640]{1,0:T(8,128)(2,1)S(1)}, bf16[640,640]{1,0:T(8,128)(2,1)}, u32[]{:S(2)}) copy-start(bf16[640,640]{1,0:T(8,128)(2,1)} %copy-done.10) | copy-start | bytes 2457604
  51.5 1.1 %copy-start.13 = (bf16[640,640]{1,0:T(8,128)(2,1)S(1)}, bf16[640,640]{1,0:T(8,128)(2,1)}, u32[]{:S(2)}) copy-start(bf16[640,640]{1,0:T(8,128)(2,1)} %copy-done.12) | copy-start | bytes 2457604
  52.6 1.1 %copy-start.15 = (bf16[640,640]{1,0:T(8,128)(2,1)S(1)}, bf16[640,640]{1,0:T(8,128)(2,1)}, u32[]{:S(2)}) copy-start(bf16[640,640]{1,0:T(8,128)(2,1)} %copy-done.14) | copy-start | bytes 2457604
  53.8 1.1 %copy-start.17 = (bf16[640,640]{1,0:T(8,128)(2,1)S(1)}, bf16[640,640]{1,0:T(8,128)(2,1)}, u32[]{:S(2)}) copy-start(bf16[640,640]{1,0:T(8,128)(2,1)} %copy-done.16) | copy-start | bytes 2457604
  54.9 1.0 copy-start.19
  92.0 12.5 %copy-start = (f32[8,160]{1,0:T(8,128)}, f32[8,160]{1,0:T(8,128)S(1)}, u32[]{:S(2)}) copy-start(f32[8,160]{1,0:T(8,128)S(1)} %get-tuple-element.37.own) | copy-start | bytes 15364

commit v2 on v1

--- a/solution.py
+++ b/solution.py
@@ -419,27 +419,24 @@
 def per_device(ham_core, halo_rows, halo_request, deriv, e_low, e_high, branches):
     row_count, order_all = ham_core.shape
     block_count = 2 * NB
-    early = (6, 3, 2, 1, 5)
+    halo = halo_rows[0, :, :, row_count:]
+    flat_deriv = deriv.reshape(3, row_count, order_all)
+    early = (1, 2, 3, 5, 6)
     late = (0, 4, 7)
-    first = halo_rows[0, early[0], :, row_count:]
-    pieces = {early[0]: passed_along(first, "dom", -block_offset(early[0]))}
-    rest, _ = lax.optimization_barrier((halo_rows, first))
-    halo = rest[0, :, :, row_count:]
-    for block in early[1:]:
-        pieces[block] = passed_along(halo[block], "dom", -block_offset(block))
-    *ready, own_row = own_part(e_high, e_low, branches, ham_core, halo_request)
-    waiting, own_row = lax.optimization_barrier(([halo[block] for block in late], own_row))
+    pieces = {block: passed_along(halo[block], "dom", -block_offset(block)) for block in early}
+    waiting, flat_deriv = lax.optimization_barrier(([halo[block] for block in late], flat_deriv))
     for block, piece in zip(late, waiting):
         pieces[block] = passed_along(piece, "dom", -block_offset(block))
     place = lax.axis_index("dom")[None].astype(jnp.int32)
+    ready = own_part(e_high, e_low, branches, ham_core, halo_request)
     density, own, mail = density_and_terms(
         place,
         e_high,
         e_low,
         branches,
         halo_request,
-        deriv.reshape(3, row_count, order_all),
-        [*ready, own_row],
+        flat_deriv,
+        ready,
         [pieces[block] for block in range(block_count)],
     )
     arrived = lax.all_to_all(mail, "dom", 0, 0, tiled=True)

time: 107 us -> 90.8 us (0.85)
  local copies, waits for them, and re-layouts: 33.5 us -> 15.1 us
  waiting for transfers between devices: 0.02 us -> 3.45 us
  blocking collectives: 12.5 us -> 9.82 us
    unnamed x40 -> x8, local copies, waits for them, and re-layouts: 17.8 us -> 0.02 us
    ppermute x8, waiting for transfers between devices: 0.02 us -> 3.45 us  [passed_along(): return lax.ppermute(value, axis, pairs)]
    all_to_all x1, blocking collectives: 12.5 us -> 9.82 us  [per_device(): arrived = lax.all_to_all(mail, 'dom', 0, 0, tiled=True)]
    squeeze x2 -> x1, local copies, waits for them, and re-layouts: 3.44 us -> 2.65 us  [per_device(): halo[block]]
  transfers between devices with their start and end apart: 8 -> 8, of which waited for: 0 -> 1; matrix products, arithmetic and copies ran while one was open for 14% -> 14% of each run, Pallas kernels for 7% -> 8%
where the time goes in v2:
time: 90.8 us; the launch traced here: 90.3 us
  Pallas kernels  46.1 us (51%)
  local copies, waits for them, and re-layouts  15.1 us (17%)
  starting transfers between devices  13.7 us (15%)
  blocking collectives  9.82 us (11%)
  waiting for transfers between devices  3.45 us (4%)
  between operations  2.04 us (2%)
    pallas_call x1, Pallas kernels, density_and_terms(): pl.pallas_call(kernel, out_shape=[jax.ShapeDtypeStruct((rows, order), jnp...  37 us
    ppermute x8, starting transfers between devices, passed_along(): return lax.ppermute(value, axis, pairs)  13.7 us
    reshape x1, local copies, waits for them, and re-layouts, per_device(): flat_deriv = deriv.reshape(3, row_count, order_all)  12.5 us
    all_to_all x1, blocking collectives, per_device(): arrived = lax.all_to_all(mail, 'dom', 0, 0, tiled=True)  9.82 us
    pallas_call x1, Pallas kernels, own_part(): pl.pallas_call(own_kernel, out_shape=[jax.ShapeDtypeStruct(*kind) for kin...  7.36 us
    ppermute x8, waiting for transfers between devices, passed_along(): return lax.ppermute(value, axis, pairs)  3.45 us
    squeeze x1, local copies, waits for them, and re-layouts, per_device(): halo[block]  2.65 us
    pallas_call x1, Pallas kernels, per_device(): pl.pallas_call(collect, out_shape=jax.ShapeDtypeStruct((3, own.shape[1]),...  1.83 us
  transfers between devices with their start and end apart: 8, of which 1 were waited for; matrix products, arithmetic and copies ran while one was open for 14% of the time, Pallas kernels for 8%

profile of v2, /device:TPU:0, one launch (start us, length us, event | category | flops | bytes accessed | tf_op | source)
XLA Modules:
  0.0 90.3 jit_solution(7221747983503025209)
XLA Ops:
  0.6 2.6 %slice_bitcast_fusion = (f32[80,640]{1,0:T(8,128)}, f32[80,640]{1,0:T(8,128)}, f32[80,640]{1,0:T(8,128)}, f32[80,640]{1,0:T(8,128)}, f32[80,640]{1,0:T(8,128)}, ...) fusion(f32[1,8,80,1280]{3,2,1,0:T(8,128)} %param.8), kind=kLoop, calls=%fused_computation | loop fusion | bytes 3276800 | tf_op jit(solution)/shard_map/squeeze | solution.py:426
  3.3 2.4 %collective-permute-start.6 = (f32[80,640]{1,0:T(8,128)}, f32[80,640]{1,0:T(8,128)S(1)}, u32[]{:S(2)}, u32[]{:S(2)}) collective-permute-start(f32[80,640]{1,0:T(8,128)} %get-tuple-element.36), channel_id=1, source_target_pairs={{0,3},{1,4},{2,5},{3,6},{4,7},{5,8},{6,9},{7,10},{8,11},{9,12},{10... | collective-permute-start | bytes 614408 | tf_op jit(solution)/shard_map/ppermute | solution.py:22
  5.7 4.6 %collective-permute-start.3 = (f32[80,640]{1,0:T(8,128)}, f32[80,640]{1,0:T(8,128)}, u32[]{:S(2)}, u32[]{:S(2)}) collective-permute-start(f32[80,640]{1,0:T(8,128)} %get-tuple-element.37), channel_id=1, source_target_pairs={{0,28},{1,29},{2,30},{3,31},{4,0},{5,1},{6,2},{7,3},{8,4},{9,5},{1... | collective-permute-start | bytes 614408 | tf_op jit(solution)/shard_map/ppermute | solution.py:22
  10.2 0.5 collective-permute-start.2
  10.8 2.3 %collective-permute-start.1 = (f32[80,640]{1,0:T(8,128)}, f32[80,640]{1,0:T(8,128)}, u32[]{:S(2)}, u32[]{:S(2)}) collective-permute-start(f32[80,640]{1,0:T(8,128)} %get-tuple-element.39), channel_id=1, source_target_pairs={{0,30},{1,31},{2,0},{3,1},{4,2},{5,3},{6,4},{7,5},{8,6},{9,7},{10,... | collective-permute-start | bytes 614408 | tf_op jit(solution)/shard_map/ppermute | solution.py:22
  13.1 0.0 collective-permute-start.5
  14.4 0.0 copy-start.1
  14.4 0.0 copy-start.2
  14.4 0.0 copy-start.3
  14.4 12.5 %reshape.23.deriv = f32[3,640,1280]{2,1,0:T(8,128)} reshape(f32[3,160,4,1280]{3,2,1,0:T(4,128)} %param.10) | data formatting | bytes 19660800 | tf_op jit(solution)/shard_map/reshape | solution.py:423
  26.9 0.0 collective-permute-done.6.refs_16_
  26.9 3.9 %collective-permute-start = (f32[80,640]{1,0:T(8,128)}, f32[80,640]{1,0:T(8,128)S(1)}, u32[]{:S(2)}, u32[]{:S(2)}) collective-permute-start(f32[80,640]{1,0:T(8,128)} %get-tuple-element.30), channel_id=1, source_target_pairs={{0,31},{1,0},{2,1},{3,2},{4,3},{5,4},{6,5},{7,6},{8,7},{9,8},{10,9... | collective-permute-start | bytes 614408 | tf_op jit(solution)/shard_map/ppermute | solution.py:22
  30.8 0.0 collective-permute-done.3.refs_13_
  30.8 0.0 collective-permute-start.4
  30.8 0.0 collective-permute-done.2.refs_12_
  30.8 0.1 collective-permute-start.7
  30.8 0.0 copy-done.1
  30.9 0.0 copy-done.2
  30.9 0.0 copy-done.3
  30.9 7.4 %shard_map.86 = (bf16[640,640]{1,0:T(8,128)(2,1)S(1)}, bf16[640,640]{1,0:T(8,128)(2,1)S(1)}, f32[640,640]{1,0:T(8,128)S(1)}, f32[640,640]{1,0:T(8,128)S(1)}, f32...) custom-call(f32[1]{0:T(128)S(6)} %copy.10.high_end, ...), custom_call_target="tpu_custom_call" | custom-call | flops 4194304000 | bytes 13000000 | tf_op jit(solution)/shard_map/pallas_call | solution.py:362
  38.2 0.0 collective-permute-done.1.refs_11_
  38.2 0.0 collective-permute-done.5.refs_15_
  38.2 0.0 collective-permute-done.refs_10_
  38.3 3.4 %collective-permute-done.4.refs_14_ = f32[80,640]{1,0:T(8,128)S(1)} collective-permute-done((f32[80,640]{1,0:T(8,128)}, f32[80,640]{1,0:T(8,128)S(1)}, u32[]{:S(2)}, u32[]{:S(2)}) %collective-permute-start.4) | collective-permute-done | bytes 204832 | tf_op jit(solution)/shard_map/ppermute | solution.py:22
  41.7 0.0 collective-permute-done.7.refs_17_
  41.7 37.0 %shard_map.87 = (f32[640,1280]{1,0:T(8,128)}, f32[8,160]{1,0:T(8,128)S(1)}, f32[32,4,128]{2,1,0:T(4,128)S(1)}) custom-call(s32[1]{0:T(128)} %bitcast.place, f32[1]{0:T(128)S(6)} %copy.10.high_end, f32[1]{0:T(128)S(6)} %copy.9.low_end, s32[5]{0:T(128)S(1)} %copy-done.3, s32[1,160]{1,0:T(1,128)S(1)} %copy-done.2, f32[3,640,1280]{2,1,0:T(8,128)} %reshape.23.deriv, ...), custom_call_target="tpu_custom_call" | custom-call | flops 37748736000 | bytes 24000000 | tf_op jit(solution)/shard_map/pallas_call | solution.py:387
  78.7 0.0 copy-start
  78.7 9.8 %all_to_all.5.mail = f32[32,4,128]{2,1,0:T(4,128)} all-to-all(f32[32,4,128]{2,1,0:T(4,128)S(1)} %get-tuple-element.34), channel_id=1, replica_groups=mesh['dom'=32] {'dom'}, dimensions={0} | all-to-all | bytes 131072 | tf_op jit(solution)/shard_map/all_to_all | solution.py:442
  88.5 0.0 copy-done
  88.5 1.8 %shard_map.88 = f32[3,160]{1,0:T(4,128)} custom-call(s32[1]{0:T(128)} %bitcast.place, f32[32,4,128]{2,1,0:T(4,128)} %all_to_all.5.mail, f32[8,160]{1,0:T(8,128)} %copy-done), custom_call_target="tpu_custom_call" | custom-call | tf_op jit(solution)/shard_map/pallas_call | solution.py:443
Async XLA Ops:
  3.3 23.6 %collective-permute-start.6 = (f32[80,640]{1,0:T(8,128)}, f32[80,640]{1,0:T(8,128)S(1)}, u32[]{:S(2)}, u32[]{:S(2)}) collective-permute-start(f32[80,640]{1,0:T(8,128)} %get-tuple-element.36), channel_id=1, source_target_pairs={{0,3},{1,4},{2,5},{3,6},{4,7},{5,8},{6,9},{7,10},{8,11},{9,12},{10... | collective-permute-start | bytes 614408 | tf_op jit(solution)/shard_map/ppermute | solution.py:22
  5.7 25.1 %collective-permute-start.3 = (f32[80,640]{1,0:T(8,128)}, f32[80,640]{1,0:T(8,128)}, u32[]{:S(2)}, u32[]{:S(2)}) collective-permute-start(f32[80,640]{1,0:T(8,128)} %get-tuple-element.37), channel_id=1, source_target_pairs={{0,28},{1,29},{2,30},{3,31},{4,0},{5,1},{6,2},{7,3},{8,4},{9,5},{1... | collective-permute-start | bytes 614408 | tf_op jit(solution)/shard_map/ppermute | solution.py:22
  10.2 20.6 %collective-permute-start.2 = (f32[80,640]{1,0:T(8,128)}, f32[80,640]{1,0:T(8,128)}, u32[]{:S(2)}, u32[]{:S(2)}) collective-permute-start(f32[80,640]{1,0:T(8,128)} %get-tuple-element.38), channel_id=1, source_target_pairs={{0,29},{1,30},{2,31},{3,0},{4,1},{5,2},{6,3},{7,4},{8,5},{9,6},{10... | collective-permute-start | bytes 614408 | tf_op jit(solution)/shard_map/ppermute | solution.py:22
  10.8 27.5 %collective-permute-start.1 = (f32[80,640]{1,0:T(8,128)}, f32[80,640]{1,0:T(8,128)}, u32[]{:S(2)}, u32[]{:S(2)}) collective-permute-start(f32[80,640]{1,0:T(8,128)} %get-tuple-element.39), channel_id=1, source_target_pairs={{0,30},{1,31},{2,0},{3,1},{4,2},{5,3},{6,4},{7,5},{8,6},{9,7},{10,... | collective-permute-start | bytes 614408 | tf_op jit(solution)/shard_map/ppermute | solution.py:22
  13.1 25.2 %collective-permute-start.5 = (f32[80,640]{1,0:T(8,128)}, f32[80,640]{1,0:T(8,128)}, u32[]{:S(2)}, u32[]{:S(2)}) collective-permute-start(f32[80,640]{1,0:T(8,128)} %get-tuple-element.43), channel_id=1, source_target_pairs={{0,2},{1,3},{2,4},{3,5},{4,6},{5,7},{6,8},{7,9},{8,10},{9,11},{10,... | collective-permute-start | bytes 614408 | tf_op jit(solution)/shard_map/ppermute | solution.py:22
  14.4 16.5 %copy-start.1 = (f32[640,1280]{1,0:T(8,128)S(1)}, f32[640,1280]{1,0:T(8,128)}, u32[]{:S(2)}) copy-start(f32[640,1280]{1,0:T(8,128)} %core.1) | copy-start | bytes 9830404
  14.4 16.5 %copy-start.2 = (s32[1,160]{1,0:T(1,128)S(1)}, s32[1,160]{1,0:T(1,128)}, u32[]{:S(2)}) copy-start(s32[1,160]{1,0:T(1,128)} %request.3) | copy-start | bytes 1924
  14.4 16.5 %copy-start.3 = (s32[5]{0:T(128)S(1)}, s32[5]{0:T(128)}, u32[]{:S(2)}) copy-start(s32[5]{0:T(128)} %branches.3) | copy-start | bytes 64
  26.9 11.4 %collective-permute-start = (f32[80,640]{1,0:T(8,128)}, f32[80,640]{1,0:T(8,128)S(1)}, u32[]{:S(2)}, u32[]{:S(2)}) collective-permute-start(f32[80,640]{1,0:T(8,128)} %get-tuple-element.30), channel_id=1, source_target_pairs={{0,31},{1,0},{2,1},{3,2},{4,3},{5,4},{6,5},{7,6},{8,7},{9,8},{10,9... | collective-permute-start | bytes 614408 | tf_op jit(solution)/shard_map/ppermute | solution.py:22
  30.8 10.9 %collective-permute-start.4 = (f32[80,640]{1,0:T(8,128)}, f32[80,640]{1,0:T(8,128)S(1)}, u32[]{:S(2)}, u32[]{:S(2)}) collective-permute-start(f32[80,640]{1,0:T(8,128)} %get-tuple-element.31), channel_id=1, source_target_pairs={{0,1},{1,2},{2,3},{3,4},{4,5},{5,6},{6,7},{7,8},{8,9},{9,10},{10,1... | collective-permute-start | bytes 614408 | tf_op jit(solution)/shard_map/ppermute | solution.py:22
  30.8 10.9 %collective-permute-start.7 = (f32[80,640]{1,0:T(8,128)}, f32[80,640]{1,0:T(8,128)S(1)}, u32[]{:S(2)}, u32[]{:S(2)}) collective-permute-start(f32[80,640]{1,0:T(8,128)} %get-tuple-element.32), channel_id=1, source_target_pairs={{0,4},{1,5},{2,6},{3,7},{4,8},{5,9},{6,10},{7,11},{8,12},{9,13},{1... | collective-permute-start | bytes 614408 | tf_op jit(solution)/shard_map/ppermute | solution.py:22
  78.7 9.8 %copy-start = (f32[8,160]{1,0:T(8,128)}, f32[8,160]{1,0:T(8,128)S(1)}, u32[]{:S(2)}) copy-start(f32[8,160]{1,0:T(8,128)S(1)} %get-tuple-element.35.own) | copy-start | bytes 15364

commit v3 on v1

--- a/solution.py
+++ b/solution.py
@@ -302,7 +302,8 @@
 
         def strip(number, total, c=c):
             at = pl.ds(pl.multiple_of(number * chunk, chunk), chunk)
-            weighted = x[at, :] * deriv_held[c, at, :]
+            some = pl.ds(pl.multiple_of(number * (chunk // ORB), chunk // ORB), chunk // ORB)
+            weighted = x[at, :] * deriv_held[c, some].reshape(chunk, order)
             row_part[at, :] = sum(weighted[:, lane : lane + SUB] for lane in range(0, order, SUB))
             return total + jnp.sum(weighted.reshape(chunk // 8, 8, order), axis=0)
 
@@ -378,7 +379,7 @@
 
 
 def density_and_terms(place, high_end, low_end, branches, request, deriv, ready, pieces):
-    rows, order = deriv.shape[1:]
+    rows, order = deriv.shape[1] * ORB, deriv.shape[3]
     atoms = rows // ORB
     vmem = pl.BlockSpec(memory_space=pltpu.VMEM)
     smem = pl.BlockSpec(memory_space=pltpu.SMEM)
@@ -404,7 +405,7 @@
             pltpu.VMEM((order, SUB), jnp.float32),
             pltpu.VMEM((order, SUB), jnp.float32),
             pltpu.VMEM((order - rows, order - rows), jnp.float32),
-            pltpu.VMEM((3, rows, order), jnp.float32),
+            pltpu.VMEM((3, atoms, ORB, order), jnp.float32),
             pltpu.VMEM((rows, SUB), jnp.float32),
             pltpu.SemaphoreType.DMA((3,)),
             pltpu.SemaphoreType.DMA,
@@ -419,14 +420,10 @@
 def per_device(ham_core, halo_rows, halo_request, deriv, e_low, e_high, branches):
     row_count, order_all = ham_core.shape
     block_count = 2 * NB
+    halo = halo_rows[0, :, :, row_count:]
     early = (6, 3, 2, 1, 5)
     late = (0, 4, 7)
-    first = halo_rows[0, early[0], :, row_count:]
-    pieces = {early[0]: passed_along(first, "dom", -block_offset(early[0]))}
-    rest, _ = lax.optimization_barrier((halo_rows, first))
-    halo = rest[0, :, :, row_count:]
-    for block in early[1:]:
-        pieces[block] = passed_along(halo[block], "dom", -block_offset(block))
+    pieces = {block: passed_along(halo[block], "dom", -block_offset(block)) for block in early}
     *ready, own_row = own_part(e_high, e_low, branches, ham_core, halo_request)
     waiting, own_row = lax.optimization_barrier(([halo[block] for block in late], own_row))
     for block, piece in zip(late, waiting):
@@ -438,7 +435,7 @@
         e_low,
         branches,
         halo_request,
-        deriv.reshape(3, row_count, order_all),
+        deriv,
         [*ready, own_row],
         [pieces[block] for block in range(block_count)],
     )

time: 107 us -> 102 us (0.953)
  local copies, waits for them, and re-layouts: 33.5 us -> 20.3 us
  waiting for transfers between devices: 0.02 us -> 10.6 us
  blocking collectives: 12.5 us -> 9.78 us
    reshape x1 -> x0, local copies, waits for them, and re-layouts: 12.2 us -> none  [per_device(): deriv.reshape(3, row_count, order_all)]
    ppermute x8, waiting for transfers between devices: 0.02 us -> 10.6 us  [passed_along(): return lax.ppermute(value, axis, pairs)]
    all_to_all x1, blocking collectives: 12.5 us -> 9.78 us  [per_device(): arrived = lax.all_to_all(mail, 'dom', 0, 0, tiled=True)]
    squeeze x2 -> x1, local copies, waits for them, and re-layouts: 3.44 us -> 2.56 us  [per_device(): halo[block]]
  transfers between devices with their start and end apart: 8 -> 8, of which waited for: 0 -> 2; matrix products, arithmetic and copies ran while one was open for 14% -> 0% of each run, Pallas kernels for 7% -> 7%
where the time goes in v3:
time: 102 us
  Pallas kernels  45.4 us (45%)
  local copies, waits for them, and re-layouts  20.3 us (20%)
  starting transfers between devices  13.7 us (13%)
  waiting for transfers between devices  10.6 us (10%)
  blocking collectives  9.78 us (10%)
  between operations  2.06 us (2%)
    pallas_call x1, Pallas kernels, density_and_terms(): pl.pallas_call(kernel, out_shape=[jax.ShapeDtypeStruct((rows, order), jnp...  36.1 us
    unnamed x40, local copies, waits for them, and re-layouts  17.7 us
    ppermute x8, starting transfers between devices, passed_along(): return lax.ppermute(value, axis, pairs)  13.7 us
    ppermute x8, waiting for transfers between devices, passed_along(): return lax.ppermute(value, axis, pairs)  10.6 us
    all_to_all x1, blocking collectives, per_device(): arrived = lax.all_to_all(mail, 'dom', 0, 0, tiled=True)  9.78 us
    pallas_call x1, Pallas kernels, own_part(): pl.pallas_call(own_kernel, out_shape=[jax.ShapeDtypeStruct(*kind) for kin...  7.4 us
    squeeze x1, local copies, waits for them, and re-layouts, per_device(): halo[block]  2.56 us
  transfers between devices with their start and end apart: 8, of which 2 were waited for; matrix products, arithmetic and copies ran while one was open for 0% of the time, Pallas kernels for 7%

profile of v3, /device:TPU:0, one launch (start us, length us, event | category | flops | bytes accessed | tf_op | source)
XLA Modules:
  0.0 101.9 jit_solution(1331165411360899667)
XLA Ops:
  0.6 0.0 copy-start.3
  0.6 0.0 copy-start.2
  0.7 0.0 copy-start.1
  0.7 2.6 %slice_bitcast_fusion = (f32[80,640]{1,0:T(8,128)S(1)}, f32[80,640]{1,0:T(8,128)S(1)}, f32[80,640]{1,0:T(8,128)S(1)}, f32[80,640]{1,0:T(8,128)}, f32[80,640]{1,0...) fusion(f32[1,8,80,1280]{3,2,1,0:T(8,128)} %param.8), kind=kLoop, calls=%fused_computation | loop fusion | bytes 3276800 | tf_op jit(solution)/shard_map/squeeze | solution.py:426
  3.2 2.4 %collective-permute-start.6 = (f32[80,640]{1,0:T(8,128)S(1)}, f32[80,640]{1,0:T(8,128)S(1)}, u32[]{:S(2)}, u32[]{:S(2)}) collective-permute-start(f32[80,640]{1,0:T(8,128)S(1)} %get-tuple-element.36), channel_id=1, source_target_pairs={{0,3},{1,4},{2,5},{3,6},{4,7},{5,8},{6,9},{7,10},{8,11},{9,12},{10... | collective-permute-start | bytes 614408 | tf_op jit(solution)/shard_map/ppermute | solution.py:22
  5.6 4.6 %collective-permute-start.3 = (f32[80,640]{1,0:T(8,128)S(1)}, f32[80,640]{1,0:T(8,128)S(1)}, u32[]{:S(2)}, u32[]{:S(2)}) collective-permute-start(f32[80,640]{1,0:T(8,128)S(1)} %get-tuple-element.37), channel_id=1, source_target_pairs={{0,28},{1,29},{2,30},{3,31},{4,0},{5,1},{6,2},{7,3},{8,4},{9,5},{1... | collective-permute-start | bytes 614408 | tf_op jit(solution)/shard_map/ppermute | solution.py:22
  10.2 0.5 collective-permute-start.2
  10.7 2.3 %collective-permute-start.1 = (f32[80,640]{1,0:T(8,128)}, f32[80,640]{1,0:T(8,128)S(1)}, u32[]{:S(2)}, u32[]{:S(2)}) collective-permute-start(f32[80,640]{1,0:T(8,128)} %get-tuple-element.39), channel_id=1, source_target_pairs={{0,30},{1,31},{2,0},{3,1},{4,2},{5,3},{6,4},{7,5},{8,6},{9,7},{10,... | collective-permute-start | bytes 614408 | tf_op jit(solution)/shard_map/ppermute | solution.py:22
  13.0 0.0 collective-permute-start.5
  14.3 0.0 copy-done.3
  14.3 0.0 copy-done.2
  14.4 0.0 copy-done.1
  14.4 7.4 %shard_map.86 = (bf16[640,640]{1,0:T(8,128)(2,1)S(1)}, bf16[640,640]{1,0:T(8,128)(2,1)S(1)}, f32[640,640]{1,0:T(8,128)S(1)}, f32[640,640]{1,0:T(8,128)S(1)}, f32...) custom-call(f32[1]{0:T(128)S(6)} %copy.10.high_end, ...), custom_call_target="tpu_custom_call" | custom-call | flops 4194304000 | bytes 13000000 | tf_op jit(solution)/shard_map/pallas_call | solution.py:363
  21.8 0.0 copy-start.4
  21.8 1.2 %copy-done.4 = f32[640,640]{1,0:T(8,128)} copy-done((f32[640,640]{1,0:T(8,128)}, f32[640,640]{1,0:T(8,128)S(1)}, u32[]{:S(2)}) %copy-start.4) | copy-done | bytes 1638424
  22.9 0.0 copy-start.6
  22.9 1.2 %copy-done.6 = f32[640,640]{1,0:T(8,128)} copy-done((f32[640,640]{1,0:T(8,128)}, f32[640,640]{1,0:T(8,128)S(1)}, u32[]{:S(2)}) %copy-start.6) | copy-done | bytes 1638424
  24.1 0.0 copy-start.8
  24.1 1.2 %copy-done.8 = f32[640,640]{1,0:T(8,128)} copy-done((f32[640,640]{1,0:T(8,128)}, f32[640,640]{1,0:T(8,128)S(1)}, u32[]{:S(2)}) %copy-start.8) | copy-done | bytes 1638424
  25.3 0.0 copy-start.10
  25.3 0.9 copy-done.10
  26.2 0.0 copy-start.12
  26.2 0.9 copy-done.12
  27.1 0.0 copy-start.14
  27.1 0.9 copy-done.14
  28.0 0.0 copy-start.16
  28.0 0.9 copy-done.16
  28.9 0.0 copy-start.18
  28.9 0.7 copy-done.18
  29.7 0.0 collective-permute-done.6.refs_16_
  29.7 3.9 %collective-permute-start = (f32[80,640]{1,0:T(8,128)}, f32[80,640]{1,0:T(8,128)S(1)}, u32[]{:S(2)}, u32[]{:S(2)}) collective-permute-start(f32[80,640]{1,0:T(8,128)} %get-tuple-element.30), channel_id=1, source_target_pairs={{0,31},{1,0},{2,1},{3,2},{4,3},{5,4},{6,5},{7,6},{8,7},{9,8},{10,9... | collective-permute-start | bytes 614408 | tf_op jit(solution)/shard_map/ppermute | solution.py:22
  33.5 0.0 collective-permute-done.3.refs_13_
  33.5 0.0 collective-permute-start.4
  33.5 0.0 collective-permute-done.2.refs_12_
  33.6 0.1 collective-permute-start.7
  33.6 0.0 collective-permute-done.1.refs_11_
  33.6 0.0 collective-permute-done.5.refs_15_
  33.6 3.5 %collective-permute-done.refs_10_ = f32[80,640]{1,0:T(8,128)S(1)} collective-permute-done((f32[80,640]{1,0:T(8,128)}, f32[80,640]{1,0:T(8,128)S(1)}, u32[]{:S(2)}, u32[]{:S(2)}) %collective-permute-start) | collective-permute-done | bytes 204832 | tf_op jit(solution)/shard_map/ppermute | solution.py:22
  37.1 7.1 %collective-permute-done.4.refs_14_ = f32[80,640]{1,0:T(8,128)S(1)} collective-permute-done((f32[80,640]{1,0:T(8,128)}, f32[80,640]{1,0:T(8,128)S(1)}, u32[]{:S(2)}, u32[]{:S(2)}) %collective-permute-start.4) | collective-permute-done | bytes 204832 | tf_op jit(solution)/shard_map/ppermute | solution.py:22
  44.3 0.0 collective-permute-done.7.refs_17_
  44.3 0.0 copy-start.5
  44.3 1.4 %copy-done.5 = f32[640,640]{1,0:T(8,128)S(1)} copy-done((f32[640,640]{1,0:T(8,128)S(1)}, f32[640,640]{1,0:T(8,128)}, u32[]{:S(2)}) %copy-start.5) | copy-done | bytes 1638424
  45.7 0.0 copy-start.7
  45.7 1.4 %copy-done.7 = f32[640,640]{1,0:T(8,128)S(1)} copy-done((f32[640,640]{1,0:T(8,128)S(1)}, f32[640,640]{1,0:T(8,128)}, u32[]{:S(2)}) %copy-start.7) | copy-done | bytes 1638424
  47.1 0.0 copy-start.9
  47.1 1.4 %copy-done.9 = f32[640,640]{1,0:T(8,128)S(1)} copy-done((f32[640,640]{1,0:T(8,128)S(1)}, f32[640,640]{1,0:T(8,128)}, u32[]{:S(2)}) %copy-start.9) | copy-done | bytes 1638424
  48.6 0.0 copy-start.11
  48.6 1.1 %copy-done.11 = bf16[640,640]{1,0:T(8,128)(2,1)S(1)} copy-done((bf16[640,640]{1,0:T(8,128)(2,1)S(1)}, bf16[640,640]{1,0:T(8,128)(2,1)}, u32[]{:S(2)}) %copy-start.11) | copy-done | bytes 819224
  49.7 0.0 copy-start.13
  49.7 1.1 %copy-done.13 = bf16[640,640]{1,0:T(8,128)(2,1)S(1)} copy-done((bf16[640,640]{1,0:T(8,128)(2,1)S(1)}, bf16[640,640]{1,0:T(8,128)(2,1)}, u32[]{:S(2)}) %copy-start.13) | copy-done | bytes 819224
  50.8 0.0 copy-start.15
  50.8 1.1 %copy-done.15 = bf16[640,640]{1,0:T(8,128)(2,1)S(1)} copy-done((bf16[640,640]{1,0:T(8,128)(2,1)S(1)}, bf16[640,640]{1,0:T(8,128)(2,1)}, u32[]{:S(2)}) %copy-start.15) | copy-done | bytes 819224
  52.0 0.0 copy-start.17
  52.0 1.1 %copy-done.17 = bf16[640,640]{1,0:T(8,128)(2,1)S(1)} copy-done((bf16[640,640]{1,0:T(8,128)(2,1)S(1)}, bf16[640,640]{1,0:T(8,128)(2,1)}, u32[]{:S(2)}) %copy-start.17) | copy-done | bytes 819224
  53.1 0.0 copy-start.19
  53.1 1.0 copy-done.19
  54.1 36.1 %shard_map.87 = (f32[640,1280]{1,0:T(8,128)}, f32[8,160]{1,0:T(8,128)S(1)}, f32[32,4,128]{2,1,0:T(4,128)S(1)}) custom-call(s32[1]{0:T(128)} %bitcast.place, f32[1]{0:T(128)S(6)} %copy.10.high_end, f32[1]{0:T(128)S(6)} %copy.9.low_end, s32[5]{0:T(128)S(1)} %copy-done.3, s32[1,160]{1,0:T(1,128)S(1)} %copy-done.2, f32[3,160,4,1280]{3,2,1,0:T(4,128)} %deriv.1, ...), custom_call_target="tpu_custom_call" | custom-call | flops 37748736000 | bytes 24000000 | tf_op jit(solution)/shard_map/pallas_call | solution.py:388
  90.3 0.0 copy-start
  90.3 9.8 %all_to_all.5.mail = f32[32,4,128]{2,1,0:T(4,128)} all-to-all(f32[32,4,128]{2,1,0:T(4,128)S(1)} %get-tuple-element.34), channel_id=1, replica_groups=mesh['dom'=32] {'dom'}, dimensions={0} | all-to-all | bytes 131072 | tf_op jit(solution)/shard_map/all_to_all | solution.py:442
  100.1 0.0 copy-done
  100.1 1.8 %shard_map.88 = f32[3,160]{1,0:T(4,128)} custom-call(s32[1]{0:T(128)} %bitcast.place, f32[32,4,128]{2,1,0:T(4,128)} %all_to_all.5.mail, f32[8,160]{1,0:T(8,128)} %copy-done), custom_call_target="tpu_custom_call" | custom-call | tf_op jit(solution)/shard_map/pallas_call | solution.py:443
Async XLA Ops:
  0.6 13.7 %copy-start.3 = (s32[5]{0:T(128)S(1)}, s32[5]{0:T(128)}, u32[]{:S(2)}) copy-start(s32[5]{0:T(128)} %branches.3) | copy-start | bytes 64
  0.6 13.7 %copy-start.2 = (s32[1,160]{1,0:T(1,128)S(1)}, s32[1,160]{1,0:T(1,128)}, u32[]{:S(2)}) copy-start(s32[1,160]{1,0:T(1,128)} %request.3) | copy-start | bytes 1924
  0.7 13.7 %copy-start.1 = (f32[640,1280]{1,0:T(8,128)S(1)}, f32[640,1280]{1,0:T(8,128)}, u32[]{:S(2)}) copy-start(f32[640,1280]{1,0:T(8,128)} %core.1) | copy-start | bytes 9830404
  3.2 26.4 %collective-permute-start.6 = (f32[80,640]{1,0:T(8,128)S(1)}, f32[80,640]{1,0:T(8,128)S(1)}, u32[]{:S(2)}, u32[]{:S(2)}) collective-permute-start(f32[80,640]{1,0:T(8,128)S(1)} %get-tuple-element.36), channel_id=1, source_target_pairs={{0,3},{1,4},{2,5},{3,6},{4,7},{5,8},{6,9},{7,10},{8,11},{9,12},{10... | collective-permute-start | bytes 614408 | tf_op jit(solution)/shard_map/ppermute | solution.py:22
  5.6 27.9 %collective-permute-start.3 = (f32[80,640]{1,0:T(8,128)S(1)}, f32[80,640]{1,0:T(8,128)S(1)}, u32[]{:S(2)}, u32[]{:S(2)}) collective-permute-start(f32[80,640]{1,0:T(8,128)S(1)} %get-tuple-element.37), channel_id=1, source_target_pairs={{0,28},{1,29},{2,30},{3,31},{4,0},{5,1},{6,2},{7,3},{8,4},{9,5},{1... | collective-permute-start | bytes 614408 | tf_op jit(solution)/shard_map/ppermute | solution.py:22
  10.2 23.4 %collective-permute-start.2 = (f32[80,640]{1,0:T(8,128)S(1)}, f32[80,640]{1,0:T(8,128)S(1)}, u32[]{:S(2)}, u32[]{:S(2)}) collective-permute-start(f32[80,640]{1,0:T(8,128)S(1)} %get-tuple-element.38), channel_id=1, source_target_pairs={{0,29},{1,30},{2,31},{3,0},{4,1},{5,2},{6,3},{7,4},{8,5},{9,6},{10... | collective-permute-start | bytes 614408 | tf_op jit(solution)/shard_map/ppermute | solution.py:22
  10.7 22.9 %collective-permute-start.1 = (f32[80,640]{1,0:T(8,128)}, f32[80,640]{1,0:T(8,128)S(1)}, u32[]{:S(2)}, u32[]{:S(2)}) collective-permute-start(f32[80,640]{1,0:T(8,128)} %get-tuple-element.39), channel_id=1, source_target_pairs={{0,30},{1,31},{2,0},{3,1},{4,2},{5,3},{6,4},{7,5},{8,6},{9,7},{10,... | collective-permute-start | bytes 614408 | tf_op jit(solution)/shard_map/ppermute | solution.py:22
  13.0 20.6 %collective-permute-start.5 = (f32[80,640]{1,0:T(8,128)}, f32[80,640]{1,0:T(8,128)S(1)}, u32[]{:S(2)}, u32[]{:S(2)}) collective-permute-start(f32[80,640]{1,0:T(8,128)} %get-tuple-element.43), channel_id=1, source_target_pairs={{0,2},{1,3},{2,4},{3,5},{4,6},{5,7},{6,8},{7,9},{8,10},{9,11},{10,... | collective-permute-start | bytes 614408 | tf_op jit(solution)/shard_map/ppermute | solution.py:22
  21.8 1.2 %copy-start.4 = (f32[640,640]{1,0:T(8,128)}, f32[640,640]{1,0:T(8,128)S(1)}, u32[]{:S(2)}) copy-start(f32[640,640]{1,0:T(8,128)S(1)} %get-tuple-element.22.refs_3_) | copy-start | bytes 4915204
  22.9 1.2 %copy-start.6 = (f32[640,640]{1,0:T(8,128)}, f32[640,640]{1,0:T(8,128)S(1)}, u32[]{:S(2)}) copy-start(f32[640,640]{1,0:T(8,128)S(1)} %get-tuple-element.23.refs_4_) | copy-start | bytes 4915204
  24.1 1.2 %copy-start.8 = (f32[640,640]{1,0:T(8,128)}, f32[640,640]{1,0:T(8,128)S(1)}, u32[]{:S(2)}) copy-start(f32[640,640]{1,0:T(8,128)S(1)} %get-tuple-element.24.refs_5_) | copy-start | bytes 4915204
  25.3 0.9 copy-start.10
  26.2 0.9 copy-start.12
  27.1 0.9 copy-start.14
  28.0 0.9 copy-start.16
  28.9 0.7 copy-start.18
  29.7 7.5 %collective-permute-start = (f32[80,640]{1,0:T(8,128)}, f32[80,640]{1,0:T(8,128)S(1)}, u32[]{:S(2)}, u32[]{:S(2)}) collective-permute-start(f32[80,640]{1,0:T(8,128)} %get-tuple-element.30), channel_id=1, source_target_pairs={{0,31},{1,0},{2,1},{3,2},{4,3},{5,4},{6,5},{7,6},{8,7},{9,8},{10,9... | collective-permute-start | bytes 614408 | tf_op jit(solution)/shard_map/ppermute | solution.py:22
  33.5 10.7 %collective-permute-start.4 = (f32[80,640]{1,0:T(8,128)}, f32[80,640]{1,0:T(8,128)S(1)}, u32[]{:S(2)}, u32[]{:S(2)}) collective-permute-start(f32[80,640]{1,0:T(8,128)} %get-tuple-element.31), channel_id=1, source_target_pairs={{0,1},{1,2},{2,3},{3,4},{4,5},{5,6},{6,7},{7,8},{8,9},{9,10},{10,1... | collective-permute-start | bytes 614408 | tf_op jit(solution)/shard_map/ppermute | solution.py:22
  33.6 10.7 %collective-permute-start.7 = (f32[80,640]{1,0:T(8,128)S(1)}, f32[80,640]{1,0:T(8,128)S(1)}, u32[]{:S(2)}, u32[]{:S(2)}) collective-permute-start(f32[80,640]{1,0:T(8,128)S(1)} %get-tuple-element.32), channel_id=1, source_target_pairs={{0,4},{1,5},{2,6},{3,7},{4,8},{5,9},{6,10},{7,11},{8,12},{9,13},{1... | collective-permute-start | bytes 614408 | tf_op jit(solution)/shard_map/ppermute | solution.py:22
  44.3 1.4 %copy-start.5 = (f32[640,640]{1,0:T(8,128)S(1)}, f32[640,640]{1,0:T(8,128)}, u32[]{:S(2)}) copy-start(f32[640,640]{1,0:T(8,128)} %copy-done.4) | copy-start | bytes 4915204
  45.7 1.4 %copy-start.7 = (f32[640,640]{1,0:T(8,128)S(1)}, f32[640,640]{1,0:T(8,128)}, u32[]{:S(2)}) copy-start(f32[640,640]{1,0:T(8,128)} %copy-done.6) | copy-start | bytes 4915204
  47.1 1.4 %copy-start.9 = (f32[640,640]{1,0:T(8,128)S(1)}, f32[640,640]{1,0:T(8,128)}, u32[]{:S(2)}) copy-start(f32[640,640]{1,0:T(8,128)} %copy-done.8) | copy-start | bytes 4915204
  48.6 1.1 %copy-start.11 = (bf16[640,640]{1,0:T(8,128)(2,1)S(1)}, bf16[640,640]{1,0:T(8,128)(2,1)}, u32[]{:S(2)}) copy-start(bf16[640,640]{1,0:T(8,128)(2,1)} %copy-done.10) | copy-start | bytes 2457604
  49.7 1.1 %copy-start.13 = (bf16[640,640]{1,0:T(8,128)(2,1)S(1)}, bf16[640,640]{1,0:T(8,128)(2,1)}, u32[]{:S(2)}) copy-start(bf16[640,640]{1,0:T(8,128)(2,1)} %copy-done.12) | copy-start | bytes 2457604
  50.8 1.1 %copy-start.15 = (bf16[640,640]{1,0:T(8,128)(2,1)S(1)}, bf16[640,640]{1,0:T(8,128)(2,1)}, u32[]{:S(2)}) copy-start(bf16[640,640]{1,0:T(8,128)(2,1)} %copy-done.14) | copy-start | bytes 2457604
  52.0 1.1 %copy-start.17 = (bf16[640,640]{1,0:T(8,128)(2,1)S(1)}, bf16[640,640]{1,0:T(8,128)(2,1)}, u32[]{:S(2)}) copy-start(bf16[640,640]{1,0:T(8,128)(2,1)} %copy-done.16) | copy-start | bytes 2457604
  53.1 1.0 copy-start.19
  90.3 9.8 %copy-start = (f32[8,160]{1,0:T(8,128)}, f32[8,160]{1,0:T(8,128)S(1)}, u32[]{:S(2)}) copy-start(f32[8,160]{1,0:T(8,128)S(1)} %get-tuple-element.35.own) | copy-start | bytes 15364

commit v4 on v3

--- a/solution.py
+++ b/solution.py
@@ -424,10 +424,13 @@
     early = (6, 3, 2, 1, 5)
     late = (0, 4, 7)
     pieces = {block: passed_along(halo[block], "dom", -block_offset(block)) for block in early}
-    *ready, own_row = own_part(e_high, e_low, branches, ham_core, halo_request)
-    waiting, own_row = lax.optimization_barrier(([halo[block] for block in late], own_row))
+    waiting, pieces[early[0]] = lax.optimization_barrier(
+        ([halo[block] for block in late], pieces[early[0]])
+    )
     for block, piece in zip(late, waiting):
         pieces[block] = passed_along(piece, "dom", -block_offset(block))
+    request, pieces[early[2]] = lax.optimization_barrier((halo_request, pieces[early[2]]))
+    ready = own_part(e_high, e_low, branches, ham_core, request)
     place = lax.axis_index("dom")[None].astype(jnp.int32)
     density, own, mail = density_and_terms(
         place,
@@ -436,7 +439,7 @@
         branches,
         halo_request,
         deriv,
-        [*ready, own_row],
+        ready,
         [pieces[block] for block in range(block_count)],
     )
     arrived = lax.all_to_all(mail, "dom", 0, 0, tiled=True)

time: 102 us -> 85.4 us (0.84)
  local copies, waits for them, and re-layouts: 20.3 us -> 2.81 us
  waiting for transfers between devices: 10.6 us -> 3.95 us
  blocking collectives: 9.78 us -> 13.9 us
  starting transfers between devices: 13.7 us -> 16.3 us
    unnamed x40 -> x8, local copies, waits for them, and re-layouts: 17.7 us -> 0.02 us
    ppermute x8, waiting for transfers between devices: 10.6 us -> 3.95 us  [passed_along(): return lax.ppermute(value, axis, pairs)]
    all_to_all x1, blocking collectives: 9.78 us -> 13.9 us  [per_device(): arrived = lax.all_to_all(mail, 'dom', 0, 0, tiled=True)]
    ppermute x8, starting transfers between devices: 13.7 us -> 16.3 us  [passed_along(): return lax.ppermute(value, axis, pairs)]
  transfers between devices with their start and end apart: 8 -> 8, of which waited for: 2 -> 2; matrix products, arithmetic and copies ran while one was open for 0% -> 0% of each run, Pallas kernels for 7% -> 9%
where the time goes in v4:
time: 85.4 us; the launch traced here: 85.2 us
  Pallas kernels  46.2 us (54%)
  starting transfers between devices  16.3 us (19%)
  blocking collectives  13.9 us (16%)
  waiting for transfers between devices  3.95 us (5%)
  local copies, waits for them, and re-layouts  2.81 us (3%)
  between operations  2.01 us (2%)
    pallas_call x1, Pallas kernels, density_and_terms(): pl.pallas_call(kernel, out_shape=[jax.ShapeDtypeStruct((rows, order), jnp...  37 us
    ppermute x8, starting transfers between devices, passed_along(): return lax.ppermute(value, axis, pairs)  16.3 us
    all_to_all x1, blocking collectives, per_device(): arrived = lax.all_to_all(mail, 'dom', 0, 0, tiled=True)  13.9 us
    pallas_call x1, Pallas kernels, own_part(): pl.pallas_call(own_kernel, out_shape=[jax.ShapeDtypeStruct(*kind) for kin...  7.35 us
    ppermute x8, waiting for transfers between devices, passed_along(): return lax.ppermute(value, axis, pairs)  3.95 us
    squeeze x1, local copies, waits for them, and re-layouts, per_device(): halo[block]  2.79 us
    pallas_call x1, Pallas kernels, per_device(): pl.pallas_call(collect, out_shape=jax.ShapeDtypeStruct((3, own.shape[1]),...  1.83 us
  transfers between devices with their start and end apart: 8, of which 2 were waited for; matrix products, arithmetic and copies ran while one was open for 0% of the time, Pallas kernels for 9%

profile of v4, /device:TPU:0, one launch (start us, length us, event | category | flops | bytes accessed | tf_op | source)
XLA Modules:
  0.0 85.2 jit_solution(16878252756059900984)
XLA Ops:
  0.6 0.0 copy-start.2
  0.6 0.0 copy-start.3
  0.7 0.0 copy-start.1
  0.7 2.8 %slice_bitcast_fusion = (f32[80,640]{1,0:T(8,128)}, f32[80,640]{1,0:T(8,128)}, f32[80,640]{1,0:T(8,128)}, f32[80,640]{1,0:T(8,128)}, f32[80,640]{1,0:T(8,128)}, ...) fusion(f32[1,8,80,1280]{3,2,1,0:T(8,128)} %param.8), kind=kLoop, calls=%fused_computation | loop fusion | bytes 3276800 | tf_op jit(solution)/shard_map/squeeze | solution.py:426
  3.5 2.4 %collective-permute-start.1 = (f32[80,640]{1,0:T(8,128)}, f32[80,640]{1,0:T(8,128)S(1)}, u32[]{:S(2)}, u32[]{:S(2)}) collective-permute-start(f32[80,640]{1,0:T(8,128)} %get-tuple-element.42), channel_id=1, source_target_pairs={{0,3},{1,4},{2,5},{3,6},{4,7},{5,8},{6,9},{7,10},{8,11},{9,12},{10... | collective-permute-start | bytes 614408 | tf_op jit(solution)/shard_map/ppermute | solution.py:22
  5.8 3.1 %collective-permute-start = (f32[80,640]{1,0:T(8,128)}, f32[80,640]{1,0:T(8,128)}, u32[]{:S(2)}, u32[]{:S(2)}) collective-permute-start(f32[80,640]{1,0:T(8,128)} %get-tuple-element.46), channel_id=1, source_target_pairs={{0,29},{1,30},{2,31},{3,0},{4,1},{5,2},{6,3},{7,4},{8,5},{9,6},{10... | collective-permute-start | bytes 614408 | tf_op jit(solution)/shard_map/ppermute | solution.py:22
  8.9 1.9 %collective-permute-start.6 = (f32[80,640]{1,0:T(8,128)}, f32[80,640]{1,0:T(8,128)}, u32[]{:S(2)}, u32[]{:S(2)}) collective-permute-start(f32[80,640]{1,0:T(8,128)} %get-tuple-element.40), channel_id=1, source_target_pairs={{0,2},{1,3},{2,4},{3,5},{4,6},{5,7},{6,8},{7,9},{8,10},{9,11},{10,... | collective-permute-start | bytes 614408 | tf_op jit(solution)/shard_map/ppermute | solution.py:22
  10.8 3.7 %collective-permute-start.3 = (f32[80,640]{1,0:T(8,128)}, f32[80,640]{1,0:T(8,128)}, u32[]{:S(2)}, u32[]{:S(2)}) collective-permute-start(f32[80,640]{1,0:T(8,128)} %get-tuple-element.41), channel_id=1, source_target_pairs={{0,30},{1,31},{2,0},{3,1},{4,2},{5,3},{6,4},{7,5},{8,6},{9,7},{10,... | collective-permute-start | bytes 614408 | tf_op jit(solution)/shard_map/ppermute | solution.py:22
  14.6 0.0 collective-permute-start.4
  15.9 0.0 collective-permute-done.1.refs_16_
  15.9 1.0 %collective-permute-start.2 = (f32[80,640]{1,0:T(8,128)}, f32[80,640]{1,0:T(8,128)S(1)}, u32[]{:S(2)}, u32[]{:S(2)}) collective-permute-start(f32[80,640]{1,0:T(8,128)} %get-tuple-element.32), channel_id=1, source_target_pairs={{0,31},{1,0},{2,1},{3,2},{4,3},{5,4},{6,5},{7,6},{8,7},{9,8},{10,9... | collective-permute-start | bytes 614408 | tf_op jit(solution)/shard_map/ppermute | solution.py:22
  16.9 0.0 collective-permute-done.refs_12_
  16.9 4.2 %collective-permute-start.5 = (f32[80,640]{1,0:T(8,128)}, f32[80,640]{1,0:T(8,128)S(1)}, u32[]{:S(2)}, u32[]{:S(2)}) collective-permute-start(f32[80,640]{1,0:T(8,128)} %get-tuple-element.34), channel_id=1, source_target_pairs={{0,1},{1,2},{2,3},{3,4},{4,5},{5,6},{6,7},{7,8},{8,9},{9,10},{10,1... | collective-permute-start | bytes 614408 | tf_op jit(solution)/shard_map/ppermute | solution.py:22
  21.1 0.0 collective-permute-done.6.refs_15_
  21.1 0.0 collective-permute-start.7
  21.1 0.0 copy-done.2
  21.1 0.0 copy-done.3
  21.1 0.0 copy-done.1
  21.1 7.4 %shard_map.86 = (bf16[640,640]{1,0:T(8,128)(2,1)S(1)}, bf16[640,640]{1,0:T(8,128)(2,1)S(1)}, f32[640,640]{1,0:T(8,128)S(1)}, f32[640,640]{1,0:T(8,128)S(1)}, f32...) custom-call(f32[1]{0:T(128)S(6)} %copy.10.high_end, ...), custom_call_target="tpu_custom_call" | custom-call | flops 4194304000 | bytes 13000000 | tf_op jit(solution)/shard_map/pallas_call | solution.py:363
  28.5 0.0 collective-permute-done.3.refs_11_
  28.5 3.5 %collective-permute-done.4.refs_13_ = f32[80,640]{1,0:T(8,128)} collective-permute-done((f32[80,640]{1,0:T(8,128)}, f32[80,640]{1,0:T(8,128)}, u32[]{:S(2)}, u32[]{:S(2)}) %collective-permute-start.4) | collective-permute-done | bytes 204832 | tf_op jit(solution)/shard_map/ppermute | solution.py:22
  32.0 0.0 collective-permute-done.2.refs_10_
  32.0 0.0 collective-permute-done.5.refs_14_
  32.0 0.5 collective-permute-done.7.refs_17_
  32.4 37.0 %shard_map.87 = (f32[640,1280]{1,0:T(8,128)}, f32[8,160]{1,0:T(8,128)S(1)}, f32[32,4,128]{2,1,0:T(4,128)S(1)}) custom-call(s32[1]{0:T(128)} %bitcast.place, f32[1]{0:T(128)S(6)} %copy.10.high_end, f32[1]{0:T(128)S(6)} %copy.9.low_end, s32[5]{0:T(128)S(1)} %copy-done.3, s32[1,160]{1,0:T(1,128)S(1)} %copy-done.2, f32[3,160,4,1280]{3,2,1,0:T(4,128)} %deriv.1, ...), custom_call_target="tpu_custom_call" | custom-call | flops 37748736000 | bytes 24000000 | tf_op jit(solution)/shard_map/pallas_call | solution.py:388
  69.5 0.0 copy-start
  69.5 13.9 %all_to_all.5.mail = f32[32,4,128]{2,1,0:T(4,128)} all-to-all(f32[32,4,128]{2,1,0:T(4,128)S(1)} %get-tuple-element.38), channel_id=1, replica_groups=mesh['dom'=32] {'dom'}, dimensions={0} | all-to-all | bytes 131072 | tf_op jit(solution)/shard_map/all_to_all | solution.py:445
  83.4 0.0 copy-done
  83.4 1.8 %shard_map.88 = f32[3,160]{1,0:T(4,128)} custom-call(s32[1]{0:T(128)} %bitcast.place, f32[32,4,128]{2,1,0:T(4,128)} %all_to_all.5.mail, f32[8,160]{1,0:T(8,128)} %copy-done), custom_call_target="tpu_custom_call" | custom-call | tf_op jit(solution)/shard_map/pallas_call | solution.py:446
Async XLA Ops:
  0.6 20.5 %copy-start.2 = (s32[1,160]{1,0:T(1,128)S(1)}, s32[1,160]{1,0:T(1,128)}, u32[]{:S(2)}) copy-start(s32[1,160]{1,0:T(1,128)} %request.2) | copy-start | bytes 1924
  0.6 20.5 %copy-start.3 = (s32[5]{0:T(128)S(1)}, s32[5]{0:T(128)}, u32[]{:S(2)}) copy-start(s32[5]{0:T(128)} %branches.3) | copy-start | bytes 64
  0.7 20.5 %copy-start.1 = (f32[640,1280]{1,0:T(8,128)S(1)}, f32[640,1280]{1,0:T(8,128)}, u32[]{:S(2)}) copy-start(f32[640,1280]{1,0:T(8,128)} %core.1) | copy-start | bytes 9830404
  3.5 12.4 %collective-permute-start.1 = (f32[80,640]{1,0:T(8,128)}, f32[80,640]{1,0:T(8,128)S(1)}, u32[]{:S(2)}, u32[]{:S(2)}) collective-permute-start(f32[80,640]{1,0:T(8,128)} %get-tuple-element.42), channel_id=1, source_target_pairs={{0,3},{1,4},{2,5},{3,6},{4,7},{5,8},{6,9},{7,10},{8,11},{9,12},{10... | collective-permute-start | bytes 614408 | tf_op jit(solution)/shard_map/ppermute | solution.py:22
  5.8 11.0 %collective-permute-start = (f32[80,640]{1,0:T(8,128)}, f32[80,640]{1,0:T(8,128)}, u32[]{:S(2)}, u32[]{:S(2)}) collective-permute-start(f32[80,640]{1,0:T(8,128)} %get-tuple-element.46), channel_id=1, source_target_pairs={{0,29},{1,30},{2,31},{3,0},{4,1},{5,2},{6,3},{7,4},{8,5},{9,6},{10... | collective-permute-start | bytes 614408 | tf_op jit(solution)/shard_map/ppermute | solution.py:22
  8.9 12.2 %collective-permute-start.6 = (f32[80,640]{1,0:T(8,128)}, f32[80,640]{1,0:T(8,128)}, u32[]{:S(2)}, u32[]{:S(2)}) collective-permute-start(f32[80,640]{1,0:T(8,128)} %get-tuple-element.40), channel_id=1, source_target_pairs={{0,2},{1,3},{2,4},{3,5},{4,6},{5,7},{6,8},{7,9},{8,10},{9,11},{10,... | collective-permute-start | bytes 614408 | tf_op jit(solution)/shard_map/ppermute | solution.py:22
  10.8 17.7 %collective-permute-start.3 = (f32[80,640]{1,0:T(8,128)}, f32[80,640]{1,0:T(8,128)}, u32[]{:S(2)}, u32[]{:S(2)}) collective-permute-start(f32[80,640]{1,0:T(8,128)} %get-tuple-element.41), channel_id=1, source_target_pairs={{0,30},{1,31},{2,0},{3,1},{4,2},{5,3},{6,4},{7,5},{8,6},{9,7},{10,... | collective-permute-start | bytes 614408 | tf_op jit(solution)/shard_map/ppermute | solution.py:22
  14.6 17.4 %collective-permute-start.4 = (f32[80,640]{1,0:T(8,128)}, f32[80,640]{1,0:T(8,128)}, u32[]{:S(2)}, u32[]{:S(2)}) collective-permute-start(f32[80,640]{1,0:T(8,128)} %get-tuple-element.47), channel_id=1, source_target_pairs={{0,28},{1,29},{2,30},{3,31},{4,0},{5,1},{6,2},{7,3},{8,4},{9,5},{1... | collective-permute-start | bytes 614408 | tf_op jit(solution)/shard_map/ppermute | solution.py:22
  15.9 16.1 %collective-permute-start.2 = (f32[80,640]{1,0:T(8,128)}, f32[80,640]{1,0:T(8,128)S(1)}, u32[]{:S(2)}, u32[]{:S(2)}) collective-permute-start(f32[80,640]{1,0:T(8,128)} %get-tuple-element.32), channel_id=1, source_target_pairs={{0,31},{1,0},{2,1},{3,2},{4,3},{5,4},{6,5},{7,6},{8,7},{9,8},{10,9... | collective-permute-start | bytes 614408 | tf_op jit(solution)/shard_map/ppermute | solution.py:22
  16.9 15.1 %collective-permute-start.5 = (f32[80,640]{1,0:T(8,128)}, f32[80,640]{1,0:T(8,128)S(1)}, u32[]{:S(2)}, u32[]{:S(2)}) collective-permute-start(f32[80,640]{1,0:T(8,128)} %get-tuple-element.34), channel_id=1, source_target_pairs={{0,1},{1,2},{2,3},{3,4},{4,5},{5,6},{6,7},{7,8},{8,9},{9,10},{10,1... | collective-permute-start | bytes 614408 | tf_op jit(solution)/shard_map/ppermute | solution.py:22
  21.1 11.3 %collective-permute-start.7 = (f32[80,640]{1,0:T(8,128)}, f32[80,640]{1,0:T(8,128)S(1)}, u32[]{:S(2)}, u32[]{:S(2)}) collective-permute-start(f32[80,640]{1,0:T(8,128)} %get-tuple-element.36), channel_id=1, source_target_pairs={{0,4},{1,5},{2,6},{3,7},{4,8},{5,9},{6,10},{7,11},{8,12},{9,13},{1... | collective-permute-start | bytes 614408 | tf_op jit(solution)/shard_map/ppermute | solution.py:22
  69.5 13.9 %copy-start = (f32[8,160]{1,0:T(8,128)}, f32[8,160]{1,0:T(8,128)S(1)}, u32[]{:S(2)}) copy-start(f32[8,160]{1,0:T(8,128)S(1)} %get-tuple-element.39.own) | copy-start | bytes 15364
